TPU v7x, 256 devices: a whole 4x4x8 slice. The times are simulated.
256 devices in a mesh: query: 32 (over y, x, core), feat: 8 (over z).
Axes of the slice: x: 4, y: 4, z: 8, core: 2. Of those that a mesh axis runs over, the one named last changes fastest.
Arguments:
- scores: float32 [262144], P(('query', 'feat')), may hold values from -6 to 6
- labels: int32 [262144], P('query'), may hold values from 0 to 4
- leaves: int32 [262144], P(('query', 'feat')), may hold values from 0 to 1023
- bins: int32 [262144, 256], P(('query', 'feat')), may hold values from 0 to 255
- lengths: int32 [32, 32], P('query'), may hold values from 1 to 1024, 8192 in all within a row
- owner: int32 [256], replicated, may hold values from 0 to 255, each once
Outputs:
- lambdas: float32 [2, 262144], P(None, ('query', 'feat'))
- leaf_values: float32 [1024], replicated
- score_step: float32 [262144], P(('query', 'feat'))
- histograms: float32 [3, 65536], P(None, ('query', 'feat'))
Inputs may be any that keep to these rules, and one draw needn't show every extreme that they name: `lengths`: each row sums to 8192. `owner`: a permutation; the p-th device of query+feat, in that order, holds the histograms of the features owner[j] for p <= j < (p + 1).
All inputs are finite; a program needn't handle non-finite values.
Results may differ from a plain program's by a relative error of at most 0.0003.
Values sent between devices are 32-bit elements; how exact they have to be, the bound alone decides.
A program may use at most 128 MiB of HBM per device.

v0:
```python
import jax
import jax.numpy as jnp
from jax import lax
from jax.sharding import PartitionSpec as P

BINS = 256
LEAVES = 1024
TILE_ROWS = 512
WINDOW = 1536


lasso_penalty = 1.0
ridge_penalty = 1.0
shrinkage = 0.1
group_width = 8


def query_of(lengths_row, count):
    bounds = jnp.cumsum(lengths_row)
    places = jnp.arange(count, dtype=jnp.int32)
    return jnp.searchsorted(bounds, places, side="right")


def place_in_query(sorted_ids):
    places = jnp.arange(sorted_ids.shape[0], dtype=jnp.int32)
    first = jnp.concatenate([jnp.ones((1,), dtype=jnp.bool_), sorted_ids[1:] != sorted_ids[:-1]])
    starts = lax.cummax(jnp.where(first, places, 0), axis=0)
    return places - starts


def query_stats(values, grades, query_ids, count):
    order = jnp.lexsort((-values, query_ids))
    ranked = place_in_query(query_ids[order])
    standing = jnp.zeros(values.shape, jnp.int32).at[order].set(ranked)
    discount = 1.0 / jnp.log2(2.0 + standing.astype(jnp.float32))
    ideal_order = jnp.lexsort((-grades, query_ids))
    ideal_ids = query_ids[ideal_order]
    ideal_place = place_in_query(ideal_ids)
    worth = jnp.exp2(grades[ideal_order].astype(jnp.float32)) - 1.0
    terms = worth / jnp.log2(2.0 + ideal_place.astype(jnp.float32))
    slots = jnp.where(ideal_ids >= 0, ideal_ids, count)
    ideal = jax.ops.segment_sum(terms, slots, num_segments=count + 1)
    usable = ideal > 0.5
    inverse = jnp.where(usable, 1.0 / jnp.where(usable, ideal, 1.0), 0.0)
    return (discount, inverse[jnp.where(query_ids >= 0, query_ids, count)])


def pair_block(row_part, col_part):
    row_score, row_grade, row_query, row_discount, row_inverse, row_place = row_part
    col_score, col_grade, col_query, col_discount, col_place = col_part
    keep = (row_query[:, None] == col_query[None, :]) & (row_query[:, None] >= 0)
    keep = keep & (col_place[None, :] > row_place[:, None])
    row_worth = jnp.exp2(row_grade.astype(jnp.float32))
    col_worth = jnp.exp2(col_grade.astype(jnp.float32))
    signs = jnp.sign(row_grade[:, None] - col_grade[None, :]).astype(jnp.float32)
    change = (
        jnp.abs(row_worth[:, None] - col_worth[None, :])
        * jnp.abs(row_discount[:, None] - col_discount[None, :])
        * row_inverse[:, None]
    )
    chance = jax.nn.sigmoid(-signs * (row_score[:, None] - col_score[None, :]))
    push = jnp.where(keep, change * chance, 0.0) * signs
    bend = jnp.where(keep, change * chance * (1.0 - chance), 0.0)
    return (
        -jnp.sum(push, axis=1),
        jnp.sum(bend, axis=1),
        jnp.sum(push, axis=0),
        jnp.sum(bend, axis=0),
    )


def add_into(total, piece, start):
    current = lax.dynamic_slice_in_dim(total, start, piece.shape[0])
    return lax.dynamic_update_slice_in_dim(total, current + piece, start, 0)


def leaf_newton(sums):
    total_grad = sums[0]
    total_curv = sums[1]
    return (
        -jnp.sign(total_grad)
        * jnp.maximum(jnp.abs(total_grad) - lasso_penalty, 0.0)
        / (total_curv + ridge_penalty)
    )


def histogram_of(gradient, curvature, bins, owner):
    weights = jnp.stack([gradient, curvature, jnp.ones_like(gradient)])
    ordered = jnp.take(bins, owner, axis=1)
    groups = ordered.shape[1] // group_width
    grouped = ordered.reshape(ordered.shape[0], groups, group_width).transpose(1, 0, 2)
    levels = jnp.arange(BINS, dtype=jnp.int32)

    def one_group(group_bins):
        onehot = (group_bins[:, :, None] == levels[None, None, :]).astype(jnp.bfloat16)
        return jnp.einsum(
            "cd,dgb->cgb", weights, onehot.astype(jnp.float32), precision=lax.Precision.HIGHEST
        )

    parts = lax.map(one_group, grouped)
    return parts.transpose(1, 0, 2, 3).reshape(3, -1)


def local(scores, labels, leaves, bins, lengths, owner):
    feat_count = lax.axis_size("feat")
    feat_pos = lax.axis_index("feat")
    own_rows = scores.shape[0]
    block_rows = labels.shape[0]
    lengths_row = lengths[0]
    queries = lengths_row.shape[0]
    block_ids = query_of(lengths_row, block_rows)
    whole = lax.all_gather(scores, "feat", axis=0, tiled=True)
    discount, inverse = query_stats(whole, labels, block_ids, queries)
    padded = (
        jnp.pad(whole, (0, WINDOW)),
        jnp.pad(labels, (0, WINDOW)),
        jnp.pad(block_ids, (0, WINDOW), constant_values=-1),
        jnp.pad(discount, (0, WINDOW)),
        jnp.pad(inverse, (0, WINDOW)),
        jnp.arange(block_rows + WINDOW, dtype=jnp.int32),
    )

    def visit(tile_index, carry):
        acc_grad, acc_curv = carry
        start = (tile_index * feat_count + feat_pos) * TILE_ROWS
        row_part = tuple((lax.dynamic_slice_in_dim(item, start, TILE_ROWS) for item in padded))
        col_part = tuple(
            (lax.dynamic_slice_in_dim(padded[which], start, WINDOW) for which in (0, 1, 2, 3, 5))
        )
        row_grad, row_curv, col_grad, col_curv = pair_block(row_part, col_part)
        acc_grad = add_into(add_into(acc_grad, col_grad, start), row_grad, start)
        acc_curv = add_into(add_into(acc_curv, col_curv, start), row_curv, start)
        return (acc_grad, acc_curv)

    empty = jnp.zeros((block_rows + WINDOW,), jnp.float32)
    acc_grad, acc_curv = lax.fori_loop(0, own_rows // TILE_ROWS, visit, (empty, empty))
    partial_sums = jnp.stack([acc_grad[:block_rows], acc_curv[:block_rows]])
    lambdas = lax.psum_scatter(partial_sums, "feat", scatter_dimension=1, tiled=True)
    table = (leaves[:, None] == jnp.arange(LEAVES, dtype=jnp.int32)[None, :]).astype(jnp.float32)
    leaf_part = jnp.dot(lambdas, table, precision=lax.Precision.HIGHEST)
    leaf_values = leaf_newton(lax.psum(leaf_part, ("query", "feat")))
    score_step = shrinkage * leaf_values[leaves]
    partial_hist = histogram_of(lambdas[0], lambdas[1], bins, owner)
    histograms = lax.psum_scatter(partial_hist, ("query", "feat"), scatter_dimension=1, tiled=True)
    return (lambdas, leaf_values, score_step, histograms)


def solution(mesh):
    in_specs = (
        P(("query", "feat")),
        P("query"),
        P(("query", "feat")),
        P(("query", "feat"), None),
        P("query", None),
        P(),
    )
    out_specs = (P(None, ("query", "feat")), P(), P(("query", "feat")), P(None, ("query", "feat")))
    return jax.shard_map(local, mesh=mesh, in_specs=in_specs, out_specs=out_specs, check_vma=False)
```

profile of v0, /device:TPU:1, one launch (start us, length us, event | category | flops | bytes accessed | tf_op | source)
XLA Modules:
  0.0 2071.5 jit_solution(8405152336099937605)
XLA Ops:
  8.9 250.6 %while.53 = (s32[]{:T(128)}, u32[8192]{0:T(1024)S(1)}, u32[8192]{0:T(1024)S(1)}, s32[32]{0:T(128)S(1)}, s32[]{:T(128)}, /*index=5*/s32[]{:T(128)}) while((s32[]{:T(128)}, u32[8192]{0:T(1024)S(1)}, u32[8192]{0:T(1024)S(1)}, s32[32]{0:T(128)S(1)}, s32[]{:T(128)}, /*index=5*/s32[]{:T(128)}) %tuple.163), condition=%wide.region_2.3_spmd.clone, body=%wide.region_1.2_spmd.clone.sunk | while | flops 1130499 | bytes 262736 | solution.py:21
  10.4 20.1 fusion.52
  30.5 20.1 fusion.51
  52.1 20.1 fusion.52
  72.3 20.1 fusion.51
  93.9 20.1 fusion.52
  114.0 20.1 fusion.51
  135.6 20.1 fusion.52
  155.8 20.1 fusion.51
  177.4 20.1 fusion.52
  197.6 20.1 fusion.51
  219.2 20.1 fusion.52
  239.3 20.1 fusion.51
  259.5 7.2 sort.47
  266.7 45.5 %gather_fusion.1 = s32[8192]{0:T(1024)S(1)} fusion(s32[8192]{0:T(1024)S(1)} %convert_element_type.47, s32[8192]{0:T(1024)S(1)} %fusion.18), kind=kCustom, calls=%fused_computation.1 | custom fusion | bytes 98304 | tf_op jit(solution)/shard_map/gather | solution.py:37
  312.3 45.5 %gather_fusion.2 = s32[8192]{0:T(1024)S(1)} fusion(s32[8192]{0:T(1024)S(1)} %copy-done, s32[8192]{0:T(1024)S(1)} %fusion.18), kind=kCustom, calls=%fused_computation.2 | custom fusion | bytes 98304 | tf_op jit(solution)/shard_map/gather | solution.py:39
  357.9 22.7 %all_gather.3 = f32[8192]{0:T(1024)S(1)} all-gather(f32[1024]{0:T(1024)S(1)} %copy-done.5), channel_id=1, replica_groups=mesh['query'=32,'feat'=8] {'feat'}, dimensions={0}, use_global_device_ids=true | all-gather | bytes 36864 | tf_op jit(solution)/shard_map/all_gather | solution.py:112
  380.6 7.5 sort.46
  388.1 45.5 %gather_fusion = s32[8192]{0:T(1024)S(1)} fusion(s32[8192]{0:T(1024)S(1)} %convert_element_type.47, s32[8192]{0:T(1024)S(1)} %get-tuple-element.414), kind=kCustom, calls=%fused_computation | custom fusion | bytes 98304 | tf_op jit(solution)/shard_map/gather | solution.py:33
  434.7 57.0 %scatter_custom_fusion.1 = f32[33]{0:T(128)S(1)} fusion(s32[8192]{0:T(1024)S(1)} %bitcast.202, f32[8192]{0:T(1024)S(1)} %fusion.23, f32[]{:T(128)} %constant.151.clone.1), kind=kCustom, calls=%fused_computation.86 | custom fusion | flops 8192 | bytes 136 | tf_op jit(solution)/shard_map/scatter-add | solution.py:42
  493.8 30.5 %scatter_custom_fusion = s32[8192]{0:T(1024)S(1)} fusion(s32[8192]{0:T(1024)S(1)} %get-tuple-element.415, s32[8192]{0:T(1024)S(1)} %bitcast_subtract_fusion.1, s32[]{:T(128)} %copy.60), kind=kCustom, calls=%fused_computation.74 | custom fusion | bytes 32772 | tf_op jit(solution)/shard_map/scatter | solution.py:34
  524.3 20.7 %select_select_fusion.4 = f32[8192]{0:T(1024)S(1)} fusion(f32[]{:T(128)} %bitcast.7, f32[]{:T(128)} %bitcast.8, f32[]{:T(128)} %bitcast.9, f32[]{:T(128)} %bitcast.10, f32[]{:T(128)} %bitcast.11, f32[]{:T(128)} %bitcast.12, f32[]{:T(128)} %bitcast.13, f32[]{:T(128)} %bitcast.14, f32[]{:T(128)} %bitcast.15, f32[]{:T(128)} %bitcast.16, f32[]{:T(128)} %bitcast.17, ...), kind=kLoop, calls=%fused_computation.66 | loop fusion | flops 573440 | bytes 65668 | tf_op jit(solution)/shard_map/gather | solution.py:45
  545.1 12.7 while.51
  546.0 4.9 fusion.46
  552.4 4.9 fusion.46
  563.4 58.4 %reduce-scatter.7.cloned.1.call-done = f32[1024,2]{1,0:T(8,128)} async-done(((f32[8192,2]{1,0:T(8,128)}), f32[1024,2]{1,0:T(8,128)}) %reduce-scatter.7.cloned.1.call-update) | async-done | bytes 8208
  623.7 102.5 %while.52 = (s32[]{:T(128)}, f32[32,3,8,256]{3,1,2,0:T(4,128)S(1)}, s32[32,1024,8]{1,2,0:T(8,128)S(1)}, f32[3,1024]{1,0:T(4,128)S(1)}, s32[]{:T(128)}) while((s32[]{:T(128)}, f32[32,3,8,256]{3,1,2,0:T(4,128)S(1)}, s32[32,1024,8]{1,2,0:T(8,128)S(1)}, f32[3,1024]{1,0:T(4,128)S(1)}, s32[]{:T(128)}) %tuple.169), condition=%wide.region_20.21_spmd.clone, body=%wide.region_19.20_spmd.clone.sunk | while | flops 77594624 | bytes 147533 | solution.py:100
  626.9 3.2 fusion.48
  630.1 3.2 fusion.48
  633.3 3.2 fusion.48
  636.5 3.2 fusion.48
  639.7 3.2 fusion.48
  642.9 3.2 fusion.48
  646.1 3.2 fusion.48
  649.3 3.2 fusion.48
  652.5 3.2 fusion.48
  655.7 3.2 fusion.48
  658.9 3.2 fusion.48
  662.1 3.2 fusion.48
  665.3 3.2 fusion.48
  668.5 3.2 fusion.48
  671.7 3.2 fusion.48
  674.9 3.2 fusion.48
  697.3 3.2 fusion.48
  726.2 16.0 copy.24
  744.7 77.6 %psum.7 = f32[2,1024]{1,0:T(2,128)S(1)} all-reduce(f32[2,1024]{1,0:T(2,128)S(1)} %fusion.15), channel_id=1, replica_groups=mesh['query'=32,'feat'=8] {'query','feat'}, use_global_device_ids=true, to_apply=%region_18.19 | all-reduce | flops 2048 | bytes 16384 | tf_op jit(solution)/shard_map/psum | solution.py:141
  822.4 4.5 gather_fusion.3
  827.5 1235.6 %reduce-scatter.9.cloned.1.call-done = f32[256,3]{1,0:T(8,128)} async-done(((f32[65536,3]{1,0:T(8,128)}), f32[256,3]{1,0:T(8,128)}) %reduce-scatter.9.cloned.1.call-update) | async-done | bytes 3088
  (170 shorter events, 76.6 us)
Async XLA Ops:
  7.2 614.7 %reduce-scatter.7.cloned.1.call-start = ((), (), s32[]{:S(2)}) async-start(), calls=%async_computation.2 | async-start | bytes 4718592
  266.7 45.6 %copy-start = (s32[8192]{0:T(1024)S(1)}, s32[8192]{0:T(1024)}, u32[]{:S(2)}) copy-start(s32[8192]{0:T(1024)} %param.13) | copy-start | bytes 98308
  312.3 45.6 %copy-start.5 = (f32[1024]{0:T(1024)S(1)}, f32[1024]{0:T(1024)}, u32[]{:S(2)}) copy-start(f32[1024]{0:T(1024)} %param.12) | copy-start | bytes 12292
  560.6 0.7 copy-start.7
  560.6 1.2 copy-start.2
  560.6 1502.4 %reduce-scatter.9.cloned.1.call-start = ((), (), s32[]{:S(2)}) async-start(), calls=%async_computation.3 | async-start | bytes 33685504
  623.1 0.6 copy-start.4
  742.2 0.7 copy-start.6
  742.2 1.1 copy-start.3
  822.4 1242.3 %copy-start.1 = (f32[1,1024]{1,0:T(1,128)}, f32[1,1024]{1,0:T(1,128)S(1)}, u32[]{:S(2)}) copy-start(f32[1,1024]{1,0:T(1,128)S(1)} %fusion.31) | copy-start | bytes 12292
Sparse Core Ops, SparseCore 0:
  560.7 61.0 reduce-scatter.6
  742.3 1320.6 reduce-scatter.8
where the time goes:
time: 2090 us; the launch traced here: 2070 us
  waiting for transfers between devices  1290 us (62%)
  other arithmetic  349 us (17%)
  local copies, waits for them, and re-layouts  210 us (10%)
  matrix products  104 us (5%)
  blocking collectives  100 us (5%)
    unnamed x4, waiting for transfers between devices  1290 us
    select_n x12, other arithmetic, query_of(): return jnp.searchsorted(bounds, places, side='right')  242 us
    dot_general x32, matrix products, one_group(): jnp.einsum('cd,dgb->cgb', weights, onehot.astype(jnp.float32), precision=...  102 us
    psum x1, blocking collectives, local(): leaf_values = leaf_newton(lax.psum(leaf_part, ('query', 'feat')))  77.6 us
    scatter-add x1, other arithmetic, query_stats(): ideal = jax.ops.segment_sum(terms, slots, num_segments=count + 1)  57 us
    gather x1, local copies, waits for them, and re-layouts, query_stats(): worth = jnp.exp2(grades[ideal_order].astype(jnp.float32)) - 1.0  45.5 us
    gather x1, local copies, waits for them, and re-layouts, query_stats(): ideal_ids = query_ids[ideal_order]  45.5 us
    gather x1, local copies, waits for them, and re-layouts, query_stats(): ranked = place_in_query(query_ids[order])  45.5 us
  transfers between devices with their start and end apart: 2, of which 2 were waited for; matrix products, arithmetic and copies ran while one was open for 0% of the time, Pallas kernels for 0%

commit v1 on v0

v1 whole, which is shorter than its diff:
```python
import jax
import jax.numpy as jnp
from jax import lax
from jax.experimental import pallas as pl
from jax.experimental.pallas import tpu as pltpu
from jax.sharding import PartitionSpec as P

BINS = 256
LEAVES = 1024
FEATURES = 256
OWN = 1024
WIN = 3 * OWN
BLOCK = 8192
QUERIES = 32
TILE = 128
TILES = WIN // TILE
OWN_TILES = OWN // TILE
STEP = 64
PEERS = 32
RING = 8
GROUP = 8
HI = 8
LO = 32

lasso_penalty = 1.0
ridge_penalty = 1.0
shrinkage = 0.1

F32 = jnp.float32
BF16 = jnp.bfloat16
MESH_ID = pl.DeviceIdType.MESH
VMEM = pl.BlockSpec(memory_space=pltpu.VMEM)
SMEM = pl.BlockSpec(memory_space=pltpu.SMEM)


def nt_dot(left, right):
    return lax.dot_general(left, right, (((1,), (1,)), ((), ())), preferred_element_type=F32)


def iota(shape, axis):
    return lax.broadcasted_iota(jnp.int32, shape, axis)


def prepare_kernel(
    scores, labels, lengths, owner, bins, rows, table, bins_t, from_left, from_right, send_sem, recv_sem
):
    feat = lax.axis_index("feat")
    query = lax.axis_index("query")
    left = lax.rem(feat + RING - 1, RING)
    right = lax.rem(feat + 1, RING)

    barrier = pltpu.get_barrier_semaphore()
    for peer in (left, right):
        pl.semaphore_signal(barrier, inc=1, device_id=(query, peer), device_id_type=MESH_ID)
    pl.semaphore_wait(barrier, 2)
    to_right = pltpu.make_async_remote_copy(
        src_ref=scores, dst_ref=from_left, send_sem=send_sem.at[0], recv_sem=recv_sem.at[0],
        device_id=(query, right), device_id_type=MESH_ID)
    to_left = pltpu.make_async_remote_copy(
        src_ref=scores, dst_ref=from_right, send_sem=send_sem.at[1], recv_sem=recv_sem.at[1],
        device_id=(query, left), device_id_type=MESH_ID)
    to_right.start()
    to_left.start()

    pick_t = (iota((FEATURES, FEATURES), 0) == owner[...]).astype(F32)
    pick = pick_t.T.astype(BF16)
    bins_t[...] = nt_dot(pick, bins[...].astype(F32).astype(BF16))

    base = (feat * OWN - OWN).astype(F32)
    length_row = jnp.broadcast_to(lengths[...].astype(F32), (QUERIES, QUERIES))
    other, one = iota((QUERIES, QUERIES), 1), iota((QUERIES, QUERIES), 0)
    starts = jnp.sum(jnp.where(other < one, length_row, 0.0), axis=1, keepdims=True)
    ends = jnp.sum(jnp.where(other <= one, length_row, 0.0), axis=1, keepdims=True)
    place = iota((1, WIN), 1).astype(F32) + base
    inside = (place >= starts) & (place < ends)
    passed = jnp.sum(jnp.where(place >= ends, 1.0, 0.0), axis=0, keepdims=True)
    ids = jnp.where(place < 0.0, -1.0, passed)

    def label_part(block):
        return labels[:, pl.ds(pl.multiple_of(block * OWN, OWN), OWN)]

    grades = jnp.concatenate([label_part(left), label_part(feat), label_part(right)], axis=1)
    worth = lax.shift_left(jnp.ones_like(grades), grades).astype(F32)

    at_least = (jnp.broadcast_to(grades, (8, WIN)) > iota((8, WIN), 0)).astype(F32).astype(BF16)
    counts = nt_dot(inside.astype(F32).astype(BF16), at_least)
    spot = iota((1, OWN), 1).astype(F32)
    gain = 1.0 / jnp.log2(2.0 + spot)
    parts = jnp.zeros((QUERIES, OWN), F32)
    for level in range(4):
        parts = parts + jnp.where(spot < counts[:, level:level + 1], gain * float(2 ** level), 0.0)
    ideal = jnp.sum(parts, axis=1, keepdims=True)
    usable = ideal > 0.5
    inverse = jnp.where(usable, 1.0 / jnp.where(usable, ideal, 1.0), 0.0)
    own_inverse = jnp.sum(jnp.where(inside, inverse, 0.0), axis=0, keepdims=True)

    def bound_at(spots, values):
        hit = (spots >= starts) & (spots < ends)
        return jnp.sum(jnp.where(hit, values, 0.0), axis=0, keepdims=True)

    zeros = jnp.zeros((1, TILE), F32)
    first = bound_at(zeros + (base + OWN), starts)
    last = bound_at(zeros + (base + 2 * OWN - 1.0), ends)
    tile_first = base + iota((1, TILE), 1).astype(F32) * TILE
    low = bound_at(jnp.maximum(tile_first, first), starts)
    high = bound_at(jnp.minimum(tile_first + (TILE - 1.0), last - 1.0), ends)
    line = iota((8, TILE), 0)
    bounds = jnp.where(line == 0, low, jnp.where(line == 1, high, jnp.where(line == 2, first, last)))
    table[...] = (bounds - base).astype(jnp.int32)

    rows[1:2, :] = ids
    rows[2:3, :] = worth
    rows[3:4, :] = own_inverse
    rows[4:8, :] = jnp.zeros((4, WIN), F32)
    to_right.wait()
    to_left.wait()
    rows[0:1, 0:OWN] = from_left[...]
    rows[0:1, OWN:2 * OWN] = scores[...]
    rows[0:1, 2 * OWN:WIN] = from_right[...]


def pair_kernel(table, rows, out, score_col, id_col, worth_col, up_col, discount_col, discount_row):
    def spread(column):
        return jnp.broadcast_to(column, (TILE, TILE))

    for tile in range(TILES):
        at = slice(tile * TILE, (tile + 1) * TILE)
        flipped = rows[:, at].T
        score_col[at, :] = spread(flipped[:, 0:1])
        id_col[at, :] = spread(flipped[:, 1:2])
        worth_col[at, :] = spread(flipped[:, 2:3])
        up_col[at, :] = spread(jnp.exp(-flipped[:, 0:1]))
    discount_row[...] = jnp.zeros_like(discount_row)

    active = table[2, 0] // TILE
    stop = (table[3, 0] + TILE - 1) // TILE

    def rank_tile(tile, carry):
        begin = pl.multiple_of(tile * TILE, TILE)
        score = jnp.broadcast_to(rows[0:1, pl.ds(begin, TILE)], (8, TILE))
        ident = jnp.broadcast_to(rows[1:2, pl.ds(begin, TILE)], (8, TILE))

        def count(start, steps, ahead, total):
            for sub in range(steps):
                spot = pl.multiple_of(start + sub * 8, 8)
                other = score_col[pl.ds(spot, 8), :]
                same = id_col[pl.ds(spot, 8), :] == ident
                if ahead is None:
                    earlier = iota((8, TILE), 0) + sub * 8 < iota((8, TILE), 1)
                    beats = (other > score) | ((other == score) & earlier)
                elif ahead:
                    beats = other >= score
                else:
                    beats = other > score
                total = total + jnp.where(same & beats, 1.0, 0.0)
            return total

        total = count(begin, TILE // 8, None, jnp.zeros((8, TILE), F32))
        total = lax.fori_loop(
            table[0, tile] // STEP, begin // STEP,
            lambda i, t: count(i * STEP, STEP // 8, True, t), total)
        total = lax.fori_loop(
            (begin + TILE) // STEP, (table[1, tile] + STEP - 1) // STEP,
            lambda i, t: count(i * STEP, STEP // 8, False, t), total)
        rank = jnp.sum(total, axis=0, keepdims=True)
        discount_row[0:1, pl.ds(begin, TILE)] = 1.0 / jnp.log2(2.0 + rank)
        return carry

    lax.fori_loop(active, stop, rank_tile, 0)

    for tile in range(TILES):
        at = slice(tile * TILE, (tile + 1) * TILE)
        flipped = discount_row[:, at].T
        discount_col[at, :] = spread(flipped[:, 0:1])

    def own_tile(index, carry):
        tile = index + OWN_TILES
        begin = pl.multiple_of(tile * TILE, TILE)

        def own(ref, line):
            return jnp.broadcast_to(ref[line:line + 1, pl.ds(begin, TILE)], (8, TILE))

        up = jnp.exp(own(rows, 0))
        ident = own(rows, 1)
        worth = own(rows, 2)
        discount = own(discount_row, 0)

        def meet(block, sums):
            grad, curv = sums
            for sub in range(STEP // 8):
                at = pl.ds(pl.multiple_of(block * STEP + sub * 8, 8), 8)
                odds = up * up_col[at, :]
                win = pltpu.reciprocal(1.0 + odds, approx=True)
                lose = odds * win
                gap = jnp.where(id_col[at, :] == ident, jnp.abs(discount - discount_col[at, :]), 0.0)
                rise = worth - worth_col[at, :]
                change = rise * gap
                grad = grad + change * jnp.where(rise > 0.0, win, lose)
                curv = curv + jnp.abs(change) * (win * lose)
            return grad, curv

        empty = jnp.zeros((8, TILE), F32)
        grad, curv = lax.fori_loop(
            table[0, tile] // STEP, (table[1, tile] + STEP - 1) // STEP, meet, (empty, empty))
        inverse = rows[3:4, pl.ds(begin, TILE)]
        spot = pl.ds(pl.multiple_of(index * TILE, TILE), TILE)
        out[0:1, spot] = -inverse * jnp.sum(grad, axis=0, keepdims=True)
        out[1:2, spot] = inverse * jnp.sum(curv, axis=0, keepdims=True)
        return carry

    lax.fori_loop(0, OWN_TILES, own_tile, 0)


def in_pieces(value, pieces):
    found = []
    for unused in range(pieces):
        piece = value.astype(BF16)
        found.append(piece)
        value = value - piece.astype(F32)
    return found


def histogram_kernel(
    lambdas, leaves, bins_t, leaf_out, step_out, hist_out,
    left_side, right_side, weights, sent, got, leaf_got, leaf_ring, chunk, chunk_got,
    send_sem, recv_sem, leaf_send, leaf_recv, ring_send, ring_recv, chunk_send, chunk_recv
):
    query = lax.axis_index("query")
    feat = lax.axis_index("feat")

    def plane_peer(offset):
        return lax.rem(query + offset, PEERS)

    def ring_peer(offset):
        return lax.rem(feat + offset, RING)

    barrier = pltpu.get_barrier_semaphore()

    @pl.loop(1, PEERS)
    def _(offset):
        pl.semaphore_signal(barrier, inc=1, device_id=(plane_peer(offset), feat), device_id_type=MESH_ID)

    @pl.loop(1, RING)
    def _(offset):
        pl.semaphore_signal(barrier, inc=1, device_id=(query, ring_peer(offset)), device_id_type=MESH_ID)

    grad, curv = lambdas[0:1, :], lambdas[1:2, :]
    leaf = leaves[...]
    leaf_row = lax.shift_right_logical(leaf, 7)
    leaf_lane = jnp.bitwise_and(leaf, 127)
    in_row = iota((8, OWN), 0) == leaf_row
    lane_hot = (iota((TILE, OWN), 0) == leaf_lane).astype(F32).astype(BF16)
    spread = []
    for value in (grad, curv):
        for piece in in_pieces(value, 3):
            spread.append(jnp.where(in_row, piece.astype(F32), 0.0).astype(BF16))
    leaf_sums = nt_dot(jnp.concatenate(spread, axis=0), lane_hot)
    leaf_got[query, 0:8, :] = leaf_sums[0:8] + leaf_sums[8:16] + leaf_sums[16:24]
    leaf_got[query, 8:16, :] = leaf_sums[24:32] + leaf_sums[32:40] + leaf_sums[40:48]

    grad_parts, curv_parts = in_pieces(grad, 2), in_pieces(curv, 2)
    stats = grad_parts + curv_parts + [jnp.ones((1, OWN), BF16)]
    for which, value in enumerate(stats):
        weights[which] = jnp.broadcast_to(value, (16, OWN))

    pl.semaphore_wait(barrier, PEERS - 1 + RING - 1)

    def leaf_copy(offset):
        return pltpu.make_async_remote_copy(
            src_ref=leaf_got.at[query], dst_ref=leaf_got.at[query],
            send_sem=leaf_send.at[offset], recv_sem=leaf_recv.at[query],
            device_id=(plane_peer(offset), feat), device_id_type=MESH_ID)

    def leaf_arrival(peer):
        return pltpu.make_async_remote_copy(
            src_ref=leaf_got.at[query], dst_ref=leaf_got.at[peer],
            send_sem=leaf_send.at[0], recv_sem=leaf_recv.at[peer],
            device_id=(peer, feat), device_id_type=MESH_ID)

    @pl.loop(1, PEERS)
    def _(offset):
        leaf_copy(offset).start()

    low_levels = iota((LO, OWN), 0).astype(F32).astype(BF16)
    high_levels = jnp.bitwise_and(iota((16, OWN), 0), 7).astype(F32).astype(BF16)
    upper = iota((16, OWN), 0) < 8
    zero = jnp.zeros((), BF16)
    unit = jnp.ones((), BF16)

    def hist_copy(offset):
        peer = plane_peer(offset)
        return pltpu.make_async_remote_copy(
            src_ref=sent.at[peer], dst_ref=got.at[query],
            send_sem=send_sem.at[offset], recv_sem=recv_sem.at[query],
            device_id=(peer, feat), device_id_type=MESH_ID)

    def hist_arrival(peer):
        return pltpu.make_async_remote_copy(
            src_ref=sent.at[peer], dst_ref=got.at[peer],
            send_sem=send_sem.at[0], recv_sem=recv_sem.at[peer],
            device_id=(peer, feat), device_id_type=MESH_ID)

    def one_group(group):
        block = bins_t[pl.ds(pl.multiple_of(group * GROUP, GROUP), GROUP), :]
        high = jnp.floor(block * (1.0 / LO))
        low = block - high * LO
        for k in range(GROUP):
            spread_low = jnp.broadcast_to(low[k:k + 1].astype(BF16), (LO, OWN))
            right_side[k * LO:(k + 1) * LO, :] = jnp.where(spread_low == low_levels, unit, zero)
        for pair in range(GROUP // 2):
            k = 2 * pair
            both = jnp.where(
                upper, jnp.broadcast_to(high[k:k + 1], (16, OWN)),
                jnp.broadcast_to(high[k + 1:k + 2], (16, OWN))).astype(BF16)
            hot = both == high_levels
            for which in range(5):
                left_side[which * 64 + pair * 16:which * 64 + (pair + 1) * 16, :] = jnp.where(
                    hot, weights[which], zero)
        full = nt_dot(left_side[...], right_side[...])
        lane = iota((HI, TILE), 1)
        for stat, whichs in enumerate(((0, 1), (2, 3), (4,))):
            for half in range(2):
                lanes = slice(half * TILE, (half + 1) * TILE)
                total = None
                for which in whichs:
                    picked = None
                    for j in range(4):
                        k = half * 4 + j
                        piece = full[which * 64 + k * HI:which * 64 + (k + 1) * HI, lanes]
                        picked = piece if j == 0 else jnp.where(lane >= j * LO, piece, picked)
                    total = picked if total is None else total + picked
                sent[group, stat * HI:(stat + 1) * HI, lanes] = total

    @pl.loop(1, PEERS // 2)
    def _(offset):
        one_group(plane_peer(offset))
        hist_copy(offset).start()

    @pl.loop(1, PEERS)
    def _(offset):
        leaf_arrival(plane_peer(offset)).wait_recv()

    def add_leaf(peer, total):
        return total + leaf_got[peer]

    leaf_ring[feat] = lax.fori_loop(0, PEERS, add_leaf, jnp.zeros((16, TILE), F32))

    def ring_copy(offset):
        return pltpu.make_async_remote_copy(
            src_ref=leaf_ring.at[feat], dst_ref=leaf_ring.at[feat],
            send_sem=ring_send.at[offset], recv_sem=ring_recv.at[feat],
            device_id=(query, ring_peer(offset)), device_id_type=MESH_ID)

    def ring_arrival(peer):
        return pltpu.make_async_remote_copy(
            src_ref=leaf_ring.at[feat], dst_ref=leaf_ring.at[peer],
            send_sem=ring_send.at[0], recv_sem=ring_recv.at[peer],
            device_id=(query, peer), device_id_type=MESH_ID)

    @pl.loop(1, RING)
    def _(offset):
        ring_copy(offset).start()

    @pl.loop(PEERS // 2, PEERS)
    def _(offset):
        one_group(plane_peer(offset))
        hist_copy(offset).start()

    one_group(query)

    @pl.loop(1, RING)
    def _(offset):
        ring_arrival(ring_peer(offset)).wait_recv()

    totals = leaf_ring[0]
    for peer in range(1, RING):
        totals = totals + leaf_ring[peer]
    total_grad, total_curv = totals[0:8], totals[8:16]
    shrunk = jnp.maximum(jnp.abs(total_grad) - lasso_penalty, 0.0) / (total_curv + ridge_penalty)
    values = jnp.where(total_grad > 0.0, -shrunk, shrunk)
    leaf_out[...] = values
    found = jnp.zeros((8, OWN), F32)
    for piece in in_pieces(values, 3):
        found = found + jnp.dot(piece, lane_hot, preferred_element_type=F32)
    step_out[...] = shrinkage * jnp.sum(jnp.where(in_row, found, 0.0), axis=0, keepdims=True)

    def add_hist(offset, total):
        peer = plane_peer(offset)
        hist_arrival(peer).wait_recv()
        return total + got[peer]

    summed = lax.fori_loop(1, PEERS, add_hist, sent[query])

    lane_block = lax.shift_right_logical(iota((GROUP, TILE), 1), 5)
    holder = iota((GROUP, TILE), 0)
    for stat in range(3):
        for half in range(2):
            moved = jnp.zeros((GROUP, TILE), F32)
            for r in range(4):
                row = stat * HI + half * 4 + r
                line = jnp.where(
                    holder < 4, jnp.broadcast_to(summed[row:row + 1, 0:TILE], (GROUP, TILE)),
                    jnp.broadcast_to(summed[row:row + 1, TILE:2 * TILE], (GROUP, TILE)))
                for kk in range(4):
                    shift = (r - kk) % 4 * LO
                    turned = pltpu.roll(line, shift, 1) if shift else line
                    moved = jnp.where((jnp.bitwise_and(holder, 3) == kk) & (lane_block == r), turned, moved)
            for k in range(GROUP):
                chunk[k, stat:stat + 1, half * TILE:(half + 1) * TILE] = moved[k:k + 1, :]
    for k in range(GROUP):
        chunk[k, 3:8, :] = jnp.zeros((5, BINS), F32)

    def chunk_copy(offset):
        peer = ring_peer(offset)
        return pltpu.make_async_remote_copy(
            src_ref=chunk.at[peer], dst_ref=chunk_got.at[feat],
            send_sem=chunk_send.at[offset], recv_sem=chunk_recv.at[feat],
            device_id=(query, peer), device_id_type=MESH_ID)

    def chunk_arrival(peer):
        return pltpu.make_async_remote_copy(
            src_ref=chunk.at[peer], dst_ref=chunk_got.at[peer],
            send_sem=chunk_send.at[0], recv_sem=chunk_recv.at[peer],
            device_id=(query, peer), device_id_type=MESH_ID)

    @pl.loop(1, RING)
    def _(offset):
        chunk_copy(offset).start()

    def add_chunk(offset, total):
        peer = ring_peer(offset)
        chunk_arrival(peer).wait_recv()
        return total + chunk_got[peer]

    final = lax.fori_loop(1, RING, add_chunk, chunk[feat])
    hist_out[...] = final[0:3]

    @pl.loop(1, PEERS)
    def _(offset):
        leaf_copy(offset).wait_send()
        hist_copy(offset).wait_send()

    @pl.loop(1, RING)
    def _(offset):
        ring_copy(offset).wait_send()
        chunk_copy(offset).wait_send()


def local(scores, labels, leaves, bins, lengths, owner):
    shape = jax.ShapeDtypeStruct
    dma = pltpu.SemaphoreType.DMA
    rows, table, bins_t = pl.pallas_call(
        prepare_kernel,
        out_shape=(
            shape((8, WIN), F32),
            shape((8, TILE), jnp.int32),
            shape((FEATURES, OWN), F32),
        ),
        in_specs=[VMEM] * 5,
        out_specs=(VMEM, VMEM, VMEM),
        scratch_shapes=[pltpu.VMEM((1, OWN), F32), pltpu.VMEM((1, OWN), F32), dma((2,)), dma((2,))],
        compiler_params=pltpu.CompilerParams(
            collective_id=1, has_side_effects=True, vmem_limit_bytes=32 * 2**20),
        name="prepare",
    )(scores.reshape(1, OWN), labels.reshape(1, BLOCK), lengths, owner.reshape(1, FEATURES), bins)
    column = pltpu.VMEM((WIN, TILE), F32)
    lambdas = pl.pallas_call(
        pair_kernel,
        out_shape=shape((2, OWN), F32),
        in_specs=[SMEM, VMEM],
        out_specs=VMEM,
        scratch_shapes=[column] * 5 + [pltpu.VMEM((8, WIN), F32)],
        compiler_params=pltpu.CompilerParams(vmem_limit_bytes=32 * 2**20),
        name="pairs",
    )(table, rows)
    leaf_values, score_step, histograms = pl.pallas_call(
        histogram_kernel,
        out_shape=(
            shape((8, TILE), F32),
            shape((1, OWN), F32),
            shape((3, BINS), F32),
        ),
        in_specs=[VMEM] * 3,
        out_specs=(VMEM, VMEM, VMEM),
        scratch_shapes=[
            pltpu.VMEM((5 * GROUP * HI, OWN), BF16),
            pltpu.VMEM((GROUP * LO, OWN), BF16),
            pltpu.VMEM((5, 16, OWN), BF16),
            pltpu.VMEM((PEERS, 3 * HI, GROUP * LO), F32),
            pltpu.VMEM((PEERS, 3 * HI, GROUP * LO), F32),
            pltpu.VMEM((PEERS, 16, TILE), F32),
            pltpu.VMEM((RING, 16, TILE), F32),
            pltpu.VMEM((RING, 8, BINS), F32),
            pltpu.VMEM((RING, 8, BINS), F32),
            dma((PEERS,)), dma((PEERS,)), dma((PEERS,)), dma((PEERS,)),
            dma((RING,)), dma((RING,)), dma((RING,)), dma((RING,)),
        ],
        compiler_params=pltpu.CompilerParams(
            collective_id=2, has_side_effects=True, vmem_limit_bytes=32 * 2**20),
        name="histograms",
    )(lambdas, leaves.reshape(1, OWN), bins_t)
    return lambdas, leaf_values.reshape(LEAVES), score_step.reshape(OWN), histograms


def solution(mesh):
    in_specs = (
        P(("query", "feat")),
        P("query"),
        P(("query", "feat")),
        P(("query", "feat"), None),
        P("query", None),
        P(),
    )
    out_specs = (P(None, ("query", "feat")), P(), P(("query", "feat")), P(None, ("query", "feat")))
    return jax.shard_map(local, mesh=mesh, in_specs=in_specs, out_specs=out_specs, check_vma=False)
```

time: 2090 us -> 58.5 us (0.03)
  waiting for transfers between devices: 1290 us -> 0 us
  other arithmetic: 349 us -> 0 us
  local copies, waits for them, and re-layouts: 210 us -> 5.14 us
  matrix products: 104 us -> 0 us
  blocking collectives: 100 us -> 0 us
  Pallas kernels: 0 us -> 51.9 us
    unnamed x4 -> x0, waiting for transfers between devices: 1290 us -> none
    select_n x16 -> x0, other arithmetic: 242 us -> none  [the longest x12 242 us: query_of(): return jnp.searchsorted(bounds, places, side='right')]
    gather x19 -> x0, local copies, waits for them, and re-layouts: 152 us -> none  [the longest x1 45.5 us: query_stats(): worth = jnp.exp2(grades[ideal_order].astype(jnp.float32)) - 1.0]
    dot_general x33 -> x0, matrix products: 104 us -> none  [the longest x32 102 us: one_group(): jnp.einsum('cd,dgb->cgb', weights, onehot.astype(jnp.float32), precision=...]
    psum x1 -> x0, blocking collectives: 77.6 us -> none  [local(): leaf_values = leaf_newton(lax.psum(leaf_part, ('query', 'feat')))]
    scatter-add x1 -> x0, other arithmetic: 57 us -> none  [query_stats(): ideal = jax.ops.segment_sum(terms, slots, num_segments=count + 1)]
    pallas_call x0 -> x3, Pallas kernels: none -> 51.9 us  [the longest x1 33.9 us: local(): pl.pallas_call(histogram_kernel, out_shape=(shape((8, TILE), F32), shape(...]
    scatter x1 -> x0, local copies, waits for them, and re-layouts: 30.5 us -> none  [query_stats(): standing = jnp.zeros(values.shape, jnp.int32).at[order].set(ranked)]
  transfers between devices with their start and end apart: 2 -> 0, of which waited for: 2 -> 0; matrix products, arithmetic and copies ran while one was open for 0% -> 0% of each run, Pallas kernels for 0% -> 0%
where the time goes in v1:
time: 58.5 us; the launch traced here: 57.7 us
  Pallas kernels  51.9 us (89%)
  local copies, waits for them, and re-layouts  5.14 us (9%)
  between operations  0.69 us (1%)
    pallas_call x1, Pallas kernels, local(): pl.pallas_call(histogram_kernel, out_shape=(shape((8, TILE), F32), shape(...  33.9 us
    pallas_call x1, Pallas kernels, local(): pl.pallas_call(pair_kernel, out_shape=shape((2, OWN), F32), in_specs=[SME...  9.8 us
    pallas_call x1, Pallas kernels, local(): pl.pallas_call(prepare_kernel, out_shape=(shape((8, WIN), F32), shape((8,...  8.17 us
    unnamed x17, local copies, waits for them, and re-layouts  5.14 us

profile of v1, /device:TPU:1, one launch (start us, length us, event | category | flops | bytes accessed | tf_op | source)
XLA Modules:
  0.0 57.7 jit_solution(16415868067748200711)
XLA Ops:
  0.6 0.0 copy-start.3
  0.6 0.0 copy-start.5
  0.7 0.0 copy-start.6
  0.7 0.7 %copy-done.3 = f32[1024]{0:T(1024)S(1)} copy-done((f32[1024]{0:T(1024)S(1)}, f32[1024]{0:T(1024)}, u32[]{:S(2)}) %copy-start.3) | copy-done | bytes 4120
  1.3 0.0 copy-done.5
  1.3 0.0 copy-done.6
  1.3 0.0 copy-start
  1.3 1.2 %copy-done = s32[1024,256]{1,0:T(8,128)S(1)} copy-done((s32[1024,256]{1,0:T(8,128)S(1)}, s32[1024,256]{1,0:T(8,128)}, u32[]{:S(2)}) %copy-start) | copy-done | bytes 1048600
  2.6 0.0 copy-start.2
  2.6 0.8 %copy-done.2 = s32[8192]{0:T(1024)S(1)} copy-done((s32[8192]{0:T(1024)S(1)}, s32[8192]{0:T(1024)}, u32[]{:S(2)}) %copy-start.2) | copy-done | bytes 32792
  3.3 8.2 %prepare.1 = (f32[8,3072]{1,0:T(8,128)S(1)}, s32[8,128]{1,0:T(8,128)S(1)}, f32[256,1024]{1,0:T(8,128)S(1)}) custom-call(f32[1,1024]{1,0:T(1,128)S(1)} %bitcast.7, s32[1,8192]{1,0:T(1,128)S(1)} %bitcast.6, s32[1,32]{1,0:T(1,128)S(1)} %copy-done.6, s32[1,256]{1,0:T(1,128)S(1)} %bitcast.11, s32[1024,256]{1,0:T(8,128)S(1)} %copy-done), custom_call_target="tpu_custom_call" | custom-call | tf_op jit(solution)/shard_map/prepare/pallas_call | solution.py:452
  11.5 0.0 copy-start.4
  11.5 9.8 %pairs.1.lambdas = f32[2,1024]{1,0:T(2,128)} custom-call(s32[8,128]{1,0:T(8,128)S(1)} %get-tuple-element.10.table, f32[8,3072]{1,0:T(8,128)S(1)} %get-tuple-element.11.rows), custom_call_target="tpu_custom_call" | custom-call | tf_op jit(solution)/shard_map/pairs/pallas_call | solution.py:467
  21.3 0.0 copy-done.4
  21.3 0.0 copy-start.1
  21.3 0.7 %copy-done.1 = f32[2,1024]{1,0:T(2,128)S(1)} copy-done((f32[2,1024]{1,0:T(2,128)S(1)}, f32[2,1024]{1,0:T(2,128)}, u32[]{:S(2)}) %copy-start.1) | copy-done | bytes 8216
  22.0 33.9 %histograms.1 = (f32[8,128]{1,0:T(8,128)S(1)}, f32[1,1024]{1,0:T(1,128)S(1)}, f32[3,256]{1,0:T(4,128)S(1)}) custom-call(f32[2,1024]{1,0:T(2,128)S(1)} %copy-done.1, s32[1,1024]{1,0:T(1,128)S(1)} %bitcast.8, f32[256,1024]{1,0:T(8,128)S(1)} %get-tuple-element.12.bins_t), custom_call_target="tpu_custom_call" | custom-call | tf_op jit(solution)/shard_map/histograms/pallas_call | solution.py:476
  56.0 0.6 %copy.13 = f32[1024]{0:T(1024)} copy(f32[1024]{0:T(1024)S(1)} %bitcast.10) | data formatting | bytes 8192
  56.6 0.6 %copy.14 = f32[1024]{0:T(1024)} copy(f32[1024]{0:T(1024)S(1)} %bitcast.9) | data formatting | bytes 8192
  57.1 0.6 %copy.15 = f32[3,256]{1,0:T(4,128)} copy(f32[3,256]{1,0:T(4,128)S(1)} %get-tuple-element.23) | data formatting | bytes 6144
Async XLA Ops:
  0.6 0.7 %copy-start.3 = (f32[1024]{0:T(1024)S(1)}, f32[1024]{0:T(1024)}, u32[]{:S(2)}) copy-start(f32[1024]{0:T(1024)} %param.6) | copy-start | bytes 12292
  0.6 0.7 %copy-start.5 = (s32[256]{0:T(256)S(1)}, s32[256]{0:T(256)}, u32[]{:S(2)}) copy-start(s32[256]{0:T(256)} %param.11) | copy-start | bytes 3076
  0.7 0.7 %copy-start.6 = (s32[1,32]{1,0:T(1,128)S(1)}, s32[1,32]{1,0:T(1,128)}, u32[]{:S(2)}) copy-start(s32[1,32]{1,0:T(1,128)} %lengths.1) | copy-start | bytes 388
  1.3 1.2 %copy-start = (s32[1024,256]{1,0:T(8,128)S(1)}, s32[1024,256]{1,0:T(8,128)}, u32[]{:S(2)}) copy-start(s32[1024,256]{1,0:T(8,128)} %bins.1) | copy-start | bytes 3145732
  2.6 0.8 %copy-start.2 = (s32[8192]{0:T(1024)S(1)}, s32[8192]{0:T(1024)}, u32[]{:S(2)}) copy-start(s32[8192]{0:T(1024)} %param.7) | copy-start | bytes 98308
  11.5 9.8 %copy-start.4 = (s32[1024]{0:T(1024)S(1)}, s32[1024]{0:T(1024)}, u32[]{:S(2)}) copy-start(s32[1024]{0:T(1024)} %param.8) | copy-start | bytes 12292
  21.3 0.7 %copy-start.1 = (f32[2,1024]{1,0:T(2,128)S(1)}, f32[2,1024]{1,0:T(2,128)}, u32[]{:S(2)}) copy-start(f32[2,1024]{1,0:T(2,128)} %pairs.1.lambdas) | copy-start | bytes 24580

commit v2 on v1

v2 whole, which is shorter than its diff:
```python
import jax
import jax.numpy as jnp
from jax import lax
from jax.experimental import pallas as pl
from jax.experimental.pallas import tpu as pltpu
from jax.sharding import PartitionSpec as P

BINS = 256
LEAVES = 1024
FEATURES = 256
OWN = 1024
WIN = 3 * OWN
BLOCK = 8192
QUERIES = 32
TILE = 128
TILES = WIN // TILE
OWN_TILES = OWN // TILE
STEP = 64
PAIR = 2 * TILE
CHIPS = 16
SIDE = 4
RING = 8
GROUP = 8
EARLY = 5
HI = 8
LO = 32

lasso_penalty = 1.0
ridge_penalty = 1.0
shrinkage = 0.1

F32 = jnp.float32
BF16 = jnp.bfloat16
MESH_ID = pl.DeviceIdType.MESH
VMEM = pl.BlockSpec(memory_space=pltpu.VMEM)
HBM = pl.BlockSpec(memory_space=pltpu.HBM)
SMEM = pl.BlockSpec(memory_space=pltpu.SMEM)


def nt_dot(left, right):
    return lax.dot_general(left, right, (((1,), (1,)), ((), ())), preferred_element_type=F32)


def iota(shape, axis):
    return lax.broadcasted_iota(jnp.int32, shape, axis)


def prepare_kernel(labels, lengths, owner, bins, rows, table, bins_t, id_col, worth_col):
    feat = lax.axis_index("feat")
    left = lax.rem(feat + RING - 1, RING)
    right = lax.rem(feat + 1, RING)

    pick_t = (iota((FEATURES, FEATURES), 0) == owner[...]).astype(F32)
    pick = pick_t.T.astype(BF16)
    bins_t[...] = nt_dot(pick, bins[...].astype(F32).astype(BF16))

    base = (feat * OWN - OWN).astype(F32)
    length_row = jnp.broadcast_to(lengths[...].astype(F32), (QUERIES, QUERIES))
    other, one = iota((QUERIES, QUERIES), 1), iota((QUERIES, QUERIES), 0)
    starts = jnp.sum(jnp.where(other < one, length_row, 0.0), axis=1, keepdims=True)
    ends = jnp.sum(jnp.where(other <= one, length_row, 0.0), axis=1, keepdims=True)
    place = iota((1, WIN), 1).astype(F32) + base
    inside = (place >= starts) & (place < ends)
    passed = jnp.sum(jnp.where(place >= ends, 1.0, 0.0), axis=0, keepdims=True)
    ids = jnp.where(place < 0.0, -1.0, passed)

    def label_part(block):
        return labels[:, pl.ds(pl.multiple_of(block * OWN, OWN), OWN)]

    grades = jnp.concatenate([label_part(left), label_part(feat), label_part(right)], axis=1)
    worth = lax.shift_left(jnp.ones_like(grades), grades).astype(F32)

    at_least = (jnp.broadcast_to(grades, (8, WIN)) > iota((8, WIN), 0)).astype(F32).astype(BF16)
    counts = nt_dot(inside.astype(F32).astype(BF16), at_least)
    spot = iota((1, OWN), 1).astype(F32)
    gain = 1.0 / jnp.log2(2.0 + spot)
    parts = jnp.zeros((QUERIES, OWN), F32)
    for level in range(4):
        parts = parts + jnp.where(spot < counts[:, level:level + 1], gain * float(2 ** level), 0.0)
    ideal = jnp.sum(parts, axis=1, keepdims=True)
    usable = ideal > 0.5
    inverse = jnp.where(usable, 1.0 / jnp.where(usable, ideal, 1.0), 0.0)
    own_inverse = jnp.sum(jnp.where(inside, inverse, 0.0), axis=0, keepdims=True)

    def bound_at(spots, values):
        hit = (spots >= starts) & (spots < ends)
        return jnp.sum(jnp.where(hit, values, 0.0), axis=0, keepdims=True)

    zeros = jnp.zeros((1, TILE), F32)
    first = bound_at(zeros + (base + OWN), starts)
    last = bound_at(zeros + (base + 2 * OWN - 1.0), ends)
    tile_first = base + iota((1, TILE), 1).astype(F32) * TILE
    low = bound_at(jnp.maximum(tile_first, first), starts)
    high = bound_at(jnp.minimum(tile_first + (TILE - 1.0), last - 1.0), ends)
    line = iota((8, TILE), 0)
    bounds = jnp.where(line == 0, low, jnp.where(line == 1, high, jnp.where(line == 2, first, last)))
    table[...] = (bounds - base).astype(jnp.int32)

    rows[...] = jnp.concatenate([ids, worth, own_inverse, own_inverse] * 2, axis=0)
    pair_lines = jnp.concatenate([ids, worth] * 4, axis=0)
    for tile in range(TILES):
        at = slice(tile * TILE, (tile + 1) * TILE)
        flipped = pair_lines[:, at].T
        id_col[at, :] = jnp.broadcast_to(flipped[:, 0:1], (TILE, TILE))
        worth_col[at, :] = jnp.broadcast_to(flipped[:, 1:2], (TILE, TILE))


def pair_kernel(
    table, from_left, scores, from_right, rows, id_col, worth_col, out, out_again,
    lines, score_col, up_col, discount_col, counts, discount_row, grads, curvs
):
    def spread(column):
        return jnp.broadcast_to(column, (TILE, TILE))

    window = jnp.concatenate([from_left[...], scores[...], from_right[...]], axis=1)
    lines[...] = jnp.concatenate([window, jnp.exp(-window), jnp.exp(window), window] * 2, axis=0)
    for tile in range(TILES):
        at = slice(tile * TILE, (tile + 1) * TILE)
        flipped = lines[:, at].T
        score_col[at, :] = spread(flipped[:, 0:1])
        up_col[at, :] = spread(flipped[:, 1:2])
    counts[...] = jnp.zeros_like(counts)

    active = table[2, 0] // PAIR
    stop = (table[3, 0] + PAIR - 1) // PAIR

    def rank_pair(pair, carry):
        begin = pl.multiple_of(pair * PAIR, PAIR)
        score = jnp.broadcast_to(lines[0:1, pl.ds(begin, PAIR)], (8, PAIR))
        ident = jnp.broadcast_to(rows[0:1, pl.ds(begin, PAIR)], (8, PAIR))

        def count(start, steps, beats, total):
            for sub in range(steps):
                spot = pl.multiple_of(start + sub * 8, 8)
                other = score_col[pl.ds(spot, 8), :]
                other_id = id_col[pl.ds(spot, 8), :]
                parts = []
                for half in range(2):
                    lanes = slice(half * TILE, (half + 1) * TILE)
                    hit = (other_id == ident[:, lanes]) & beats(other, score[:, lanes], half, sub)
                    parts.append(total[half] + jnp.where(hit, 1.0, 0.0))
                total = tuple(parts)
            return total

        def ahead(other, own, half, sub):
            return other >= own

        def behind(other, own, half, sub):
            return other > own

        def around(other, own, half, sub):
            if sub * 8 < half * TILE:
                return other >= own
            if sub * 8 >= (half + 1) * TILE:
                return other > own
            earlier = iota((8, TILE), 0) + (sub * 8 - half * TILE) < iota((8, TILE), 1)
            return (other > own) | ((other == own) & earlier)

        empty = jnp.zeros((8, TILE), F32)
        total = count(begin, PAIR // 8, around, (empty, empty))
        total = lax.fori_loop(
            table[0, 2 * pair] // STEP, begin // STEP,
            lambda i, t: count(i * STEP, STEP // 8, ahead, t), total)
        total = lax.fori_loop(
            (begin + PAIR) // STEP, (table[1, 2 * pair + 1] + STEP - 1) // STEP,
            lambda i, t: count(i * STEP, STEP // 8, behind, t), total)
        counts[:, pl.ds(begin, PAIR)] = jnp.concatenate(total, axis=1)
        return carry

    lax.fori_loop(active, stop, rank_pair, 0)

    rank = jnp.broadcast_to(jnp.sum(counts[...], axis=0, keepdims=True), (8, WIN))
    discount = 1.0 / jnp.log2(2.0 + rank)
    discount_row[...] = discount
    for tile in range(TILES):
        at = slice(tile * TILE, (tile + 1) * TILE)
        discount_col[at, :] = spread(discount[:, at].T[:, 0:1])

    def own_pair(index, carry):
        pair = index + OWN // PAIR
        begin = pl.multiple_of(pair * PAIR, PAIR)

        def own(ref, line):
            return jnp.broadcast_to(ref[line:line + 1, pl.ds(begin, PAIR)], (8, PAIR))

        up = -own(lines, 2)
        ident = own(rows, 0)
        worth = own(rows, 1)
        discount = discount_row[:, pl.ds(begin, PAIR)]

        def meet(block, sums):
            for sub in range(STEP // 8):
                at = pl.ds(pl.multiple_of(block * STEP + sub * 8, 8), 8)
                other_up, other_id = up_col[at, :], id_col[at, :]
                other_discount, other_worth = discount_col[at, :], worth_col[at, :]
                parts = []
                for half in range(2):
                    lanes = slice(half * TILE, (half + 1) * TILE)
                    odds = up[:, lanes] * other_up
                    win = pltpu.reciprocal(1.0 - odds, approx=True)
                    lose = odds * win
                    gap = jnp.where(other_id == ident[:, lanes], discount[:, lanes] - other_discount, 0.0)
                    rise = worth[:, lanes] - other_worth
                    change = jnp.abs(rise * gap)
                    parts.append(sums[half][0] + change * jnp.where(rise > 0.0, win, lose))
                    parts.append(sums[half][1] + change * (win * lose))
                sums = ((parts[0], parts[1]), (parts[2], parts[3]))
            return sums

        empty = jnp.zeros((8, TILE), F32)
        sums = lax.fori_loop(
            table[0, 2 * pair] // STEP, (table[1, 2 * pair + 1] + STEP - 1) // STEP, meet,
            ((empty, empty), (empty, empty)))
        for half in range(2):
            spot = pl.ds(pl.multiple_of(index * PAIR + half * TILE, TILE), TILE)
            grads[:, spot] = sums[half][0]
            curvs[:, spot] = sums[half][1]
        return carry

    lax.fori_loop(0, OWN // PAIR, own_pair, 0)
    inverse = -rows[2:3, OWN:2 * OWN]
    both = jnp.concatenate([
        inverse * jnp.sum(grads[...], axis=0, keepdims=True),
        inverse * jnp.sum(curvs[...], axis=0, keepdims=True)], axis=0)
    out[...] = both
    out_again[...] = both


def in_pieces(value, pieces):
    found = []
    for unused in range(pieces):
        piece = value.astype(BF16)
        found.append(piece)
        value = value - piece.astype(F32)
    return found


def histogram_kernel(
    lambdas, leaves, bins_t, leaf_out, step_out, hist_out,
    left_side, right_side, weights, pair_sent, pair_got, sent, got,
    leaf_mine, leaf_pair, leaf_got, leaf_ring, leaf_both, chunk, chunk_got,
    pair_send, pair_recv, send_sem, recv_sem, leaf_send, leaf_recv, ring_send, ring_recv,
    chunk_send, chunk_recv, one_send, one_recv
):
    query = lax.axis_index("query")
    feat = lax.axis_index("feat")
    core = lax.rem(query, 2)
    chip = lax.div(query, 2)
    other_core = 1 - core
    sibling = chip * 2 + other_core
    chip_y, chip_x = lax.div(chip, SIDE), lax.rem(chip, SIDE)

    def chip_peer(offset):
        return lax.rem(chip_y + lax.div(offset, SIDE), SIDE) * SIDE + lax.rem(chip_x + lax.rem(offset, SIDE), SIDE)

    def ring_peer(offset):
        return lax.rem(feat + offset, RING)

    def remote(source, target, send, recv, device):
        return pltpu.make_async_remote_copy(
            src_ref=source, dst_ref=target, send_sem=send, recv_sem=recv, device_id=device, device_id_type=MESH_ID)

    barrier = pltpu.get_barrier_semaphore()
    pl.semaphore_signal(barrier, inc=1, device_id=(sibling, feat), device_id_type=MESH_ID)

    @pl.loop(1, CHIPS)
    def _(offset):
        pl.semaphore_signal(barrier, inc=1, device_id=(chip_peer(offset) * 2 + core, feat), device_id_type=MESH_ID)

    @pl.loop(1, RING)
    def _(offset):
        pl.semaphore_signal(barrier, inc=1, device_id=(query, ring_peer(offset)), device_id_type=MESH_ID)

    grad, curv = lambdas[0:1, :], lambdas[1:2, :]
    leaf = leaves[...]
    leaf_row = lax.shift_right_logical(leaf, 7)
    leaf_lane = jnp.bitwise_and(leaf, 127)
    in_row = iota((8, OWN), 0) == leaf_row
    lane_hot = (iota((TILE, OWN), 0) == leaf_lane).astype(F32).astype(BF16)
    spread = []
    for value in (grad, curv):
        for piece in in_pieces(value, 3):
            spread.append(jnp.where(in_row, piece.astype(F32), 0.0).astype(BF16))
    leaf_sums = nt_dot(jnp.concatenate(spread, axis=0), lane_hot)
    leaf_mine[0] = leaf_sums[0:8] + leaf_sums[8:16] + leaf_sums[16:24]
    leaf_mine[1] = leaf_sums[24:32] + leaf_sums[32:40] + leaf_sums[40:48]
    chunk[...] = jnp.zeros_like(chunk)

    stats = in_pieces(grad, 2) + in_pieces(curv, 2) + [jnp.ones((1, OWN), BF16)]
    for which, value in enumerate(stats):
        weights[which] = jnp.broadcast_to(value, (16, OWN))

    low_levels = iota((LO, OWN), 0).astype(F32).astype(BF16)
    high_levels = jnp.bitwise_and(iota((16, OWN), 0), 7).astype(F32).astype(BF16)
    upper = iota((16, OWN), 0) < 8
    zero = jnp.zeros((), BF16)
    unit = jnp.ones((), BF16)

    def one_hots(group, slot):
        block = bins_t[pl.ds(pl.multiple_of(group * GROUP, GROUP), GROUP), :]
        high = jnp.floor(block * (1.0 / LO))
        low = block - high * LO
        for k in range(GROUP):
            spread_low = jnp.broadcast_to(low[k:k + 1].astype(BF16), (LO, OWN))
            right_side[slot, k * LO:(k + 1) * LO, :] = jnp.where(spread_low == low_levels, unit, zero)
        for pair in range(GROUP // 2):
            k = 2 * pair
            both = jnp.where(
                upper, jnp.broadcast_to(high[k:k + 1], (16, OWN)),
                jnp.broadcast_to(high[k + 1:k + 2], (16, OWN))).astype(BF16)
            hot = both == high_levels
            for which in range(5):
                left_side[slot, which * 64 + pair * 16:which * 64 + (pair + 1) * 16, :] = jnp.where(
                    hot, weights[which], zero)

    def sums(slot, target, index):
        full = nt_dot(left_side[slot], right_side[slot])
        lane = iota((HI, TILE), 1)
        for stat, whichs in enumerate(((0, 1), (2, 3), (4,))):
            for half in range(2):
                lanes = slice(half * TILE, (half + 1) * TILE)
                total = None
                for which in whichs:
                    picked = None
                    for j in range(4):
                        k = half * 4 + j
                        piece = full[which * 64 + k * HI:which * 64 + (k + 1) * HI, lanes]
                        picked = piece if j == 0 else jnp.where(lane >= j * LO, piece, picked)
                    total = picked if total is None else total + picked
                target[index, stat * HI:(stat + 1) * HI, lanes] = total

    def chip_at(turn):
        return chip_peer(lax.rem(turn + 1, CHIPS))

    def both_groups(turn):
        peer = chip_at(turn)
        one_hots(peer * 2 + other_core, 0)
        one_hots(peer * 2 + core, 1)
        sums(0, pair_sent, peer)
        sums(1, sent, peer)

    def pair_copy(turn):
        peer = chip_at(turn)
        return remote(pair_sent.at[peer], pair_got.at[peer], pair_send.at[peer], pair_recv.at[peer], (sibling, feat))

    def plane_copy(offset):
        peer = chip_peer(offset)
        return remote(sent.at[peer], got.at[chip], send_sem.at[peer], recv_sem.at[chip], (peer * 2 + core, feat))

    def plane_arrival(offset):
        peer = chip_peer(offset)
        return remote(sent.at[peer], got.at[peer], send_sem.at[peer], recv_sem.at[peer], (peer * 2 + core, feat))

    def join(turn):
        pair_copy(turn).wait_recv()
        peer = chip_at(turn)
        sent[peer] = sent[peer] + pair_got[peer]

    @pl.loop(0, EARLY)
    def _(turn):
        both_groups(turn)

    pl.semaphore_wait(barrier, 1 + CHIPS - 1 + RING - 1)

    leaf_swap = remote(leaf_mine.at[other_core], leaf_pair, one_send.at[0], one_recv.at[0], (sibling, feat))
    leaf_swap.start()

    @pl.loop(0, EARLY)
    def _(turn):
        pair_copy(turn).start()

    both_groups(EARLY)
    pair_copy(EARLY).start()
    both_groups(EARLY + 1)
    pair_copy(EARLY + 1).start()

    @pl.loop(1, EARLY + 1)
    def _(turn):
        join(turn - 1)
        plane_copy(turn).start()

    leaf_swap.wait_recv()
    leaf_got[chip] = leaf_mine[core] + leaf_pair[...]

    def leaf_copy(offset):
        peer = chip_peer(offset)
        return remote(leaf_got.at[chip], leaf_got.at[chip], leaf_send.at[peer], leaf_recv.at[chip], (peer * 2 + core, feat))

    def leaf_arrival(offset):
        peer = chip_peer(offset)
        return remote(leaf_got.at[chip], leaf_got.at[peer], leaf_send.at[peer], leaf_recv.at[peer], (peer * 2 + core, feat))

    @pl.loop(1, CHIPS)
    def _(offset):
        leaf_copy(offset).start()

    @pl.loop(EARLY + 2, CHIPS)
    def _(turn):
        both_groups(turn)
        pair_copy(turn).start()
        join(turn - 2)
        plane_copy(turn - 1).start()

    join(CHIPS - 2)
    plane_copy(CHIPS - 1).start()
    join(CHIPS - 1)

    @pl.loop(1, CHIPS)
    def _(offset):
        leaf_arrival(offset).wait_recv()

    leaf_ring[feat] = lax.fori_loop(
        0, CHIPS, lambda peer, total: total + leaf_got[peer], jnp.zeros((8, TILE), F32))

    def ring_copy(offset):
        peer = ring_peer(offset)
        return remote(leaf_ring.at[feat], leaf_ring.at[feat], ring_send.at[peer], ring_recv.at[feat], (query, peer))

    def ring_arrival(offset):
        peer = ring_peer(offset)
        return remote(leaf_ring.at[feat], leaf_ring.at[peer], ring_send.at[peer], ring_recv.at[peer], (query, peer))

    @pl.loop(1, RING)
    def _(offset):
        ring_copy(offset).start()

    def add_hist(offset, total):
        plane_arrival(offset).wait_recv()
        return total + got[chip_peer(offset)]

    summed = lax.fori_loop(1, CHIPS, add_hist, sent[chip])

    lane_block = lax.shift_right_logical(iota((GROUP, TILE), 1), 5)
    holder = iota((GROUP, TILE), 0)
    for stat in range(3):
        for half in range(2):
            moved = jnp.zeros((GROUP, TILE), F32)
            for r in range(4):
                row = stat * HI + half * 4 + r
                line = jnp.where(
                    holder < 4, jnp.broadcast_to(summed[row:row + 1, 0:TILE], (GROUP, TILE)),
                    jnp.broadcast_to(summed[row:row + 1, TILE:2 * TILE], (GROUP, TILE)))
                for kk in range(4):
                    shift = (r - kk) % 4 * LO
                    turned = pltpu.roll(line, shift, 1) if shift else line
                    moved = jnp.where((jnp.bitwise_and(holder, 3) == kk) & (lane_block == r), turned, moved)
            line = stat * 2 + half
            for k in range(GROUP):
                chunk[k, line:line + 1, :] = moved[k:k + 1, :]

    def chunk_copy(offset):
        peer = ring_peer(offset)
        return remote(chunk.at[peer], chunk_got.at[feat], chunk_send.at[peer], chunk_recv.at[feat], (query, peer))

    def chunk_arrival(offset):
        peer = ring_peer(offset)
        return remote(chunk.at[peer], chunk_got.at[peer], chunk_send.at[peer], chunk_recv.at[peer], (query, peer))

    @pl.loop(1, RING)
    def _(offset):
        chunk_copy(offset).start()

    @pl.loop(1, RING)
    def _(offset):
        ring_arrival(offset).wait_recv()

    half_total = leaf_ring[0]
    for peer in range(1, RING):
        half_total = half_total + leaf_ring[peer]
    leaf_both[core] = half_total
    leaf_back = remote(leaf_both.at[core], leaf_both.at[core], one_send.at[1], one_recv.at[1], (sibling, feat))
    leaf_back.start()

    leaf_back_here = remote(
        leaf_both.at[core], leaf_both.at[other_core], one_send.at[1], one_recv.at[1], (sibling, feat))
    leaf_back_here.wait_recv()
    total_grad, total_curv = leaf_both[0], leaf_both[1]
    shrunk = jnp.maximum(jnp.abs(total_grad) - lasso_penalty, 0.0) / (total_curv + ridge_penalty)
    values = jnp.where(total_grad > 0.0, -shrunk, shrunk)
    leaf_out[...] = values
    found = jnp.zeros((8, OWN), F32)
    for piece in in_pieces(values, 3):
        found = found + jnp.dot(piece, lane_hot, preferred_element_type=F32)
    step_out[...] = shrinkage * jnp.sum(jnp.where(in_row, found, 0.0), axis=0, keepdims=True)

    def add_chunk(offset, total):
        chunk_arrival(offset).wait_recv()
        return total + chunk_got[ring_peer(offset)]

    hist_out[...] = lax.fori_loop(1, RING, add_chunk, chunk[feat])

    leaf_swap.wait_send()
    leaf_back.wait_send()
    pair_copy(CHIPS - 1).wait_send()

    @pl.loop(1, CHIPS)
    def _(offset):
        pair_copy(offset - 1).wait_send()
        plane_copy(offset).wait_send()
        leaf_copy(offset).wait_send()

    @pl.loop(1, RING)
    def _(offset):
        ring_copy(offset).wait_send()
        chunk_copy(offset).wait_send()


def finish_kernel(leaf_in, step_in, hist_in, leaf_out, step_out, hist_out, hist, sem):
    for stat in range(3):
        for half in range(2):
            line = stat * 2 + half
            hist[stat:stat + 1, half * TILE:(half + 1) * TILE] = hist_in[line:line + 1, :]
    copies = [
        pltpu.make_async_copy(source, target, sem.at[which])
        for which, (source, target) in enumerate(((leaf_in, leaf_out), (step_in, step_out), (hist, hist_out)))]
    for copy in copies:
        copy.start()
    for copy in copies:
        copy.wait()


def local(scores, labels, leaves, bins, lengths, owner):
    shape = jax.ShapeDtypeStruct
    dma = pltpu.SemaphoreType.DMA
    column = pltpu.VMEM((WIN, TILE), F32)
    ring = [(place, (place + 1) % RING) for place in range(RING)]
    from_left = lax.ppermute(scores, "feat", ring)
    from_right = lax.ppermute(scores, "feat", [(there, here) for here, there in ring])
    rows, table, bins_t, id_col, worth_col = pl.pallas_call(
        prepare_kernel,
        out_shape=(
            shape((8, WIN), F32),
            shape((8, TILE), jnp.int32),
            shape((FEATURES, OWN), F32),
            shape((WIN, TILE), F32),
            shape((WIN, TILE), F32),
        ),
        in_specs=[VMEM] * 4,
        out_specs=(VMEM,) * 5,
        cost_estimate=pl.CostEstimate(flops=2**30, bytes_accessed=2**23, transcendentals=0),
        compiler_params=pltpu.CompilerParams(vmem_limit_bytes=32 * 2**20),
        name="prepare",
    )(labels.reshape(1, BLOCK), lengths, owner.reshape(1, FEATURES), bins)
    lambdas, lambdas_again = pl.pallas_call(
        pair_kernel,
        out_shape=(shape((2, OWN), F32), shape((2, OWN), F32)),
        in_specs=[SMEM] + [VMEM] * 6,
        out_specs=(VMEM, VMEM),
        scratch_shapes=[pltpu.VMEM((8, WIN), F32)] + [column] * 3 + [pltpu.VMEM((8, WIN), F32)] * 2 + [pltpu.VMEM((8, OWN), F32)] * 2,
        compiler_params=pltpu.CompilerParams(vmem_limit_bytes=32 * 2**20),
        name="pairs",
    )(table, from_left.reshape(1, OWN), scores.reshape(1, OWN), from_right.reshape(1, OWN), rows, id_col, worth_col)
    part = pltpu.VMEM((CHIPS, 3 * HI, GROUP * LO), F32)
    leaf_values, score_step, histograms = pl.pallas_call(
        histogram_kernel,
        out_shape=(
            shape((8, TILE), F32),
            shape((1, OWN), F32),
            shape((8, TILE), F32),
        ),
        in_specs=[VMEM] * 3,
        out_specs=(VMEM, VMEM, VMEM),
        scratch_shapes=[
            pltpu.VMEM((2, 5 * GROUP * HI, OWN), BF16),
            pltpu.VMEM((2, GROUP * LO, OWN), BF16),
            pltpu.VMEM((5, 16, OWN), BF16),
            part, part, part, part,
            pltpu.VMEM((2, 8, TILE), F32),
            pltpu.VMEM((8, TILE), F32),
            pltpu.VMEM((CHIPS, 8, TILE), F32),
            pltpu.VMEM((RING, 8, TILE), F32),
            pltpu.VMEM((2, 8, TILE), F32),
            pltpu.VMEM((RING, 8, TILE), F32),
            pltpu.VMEM((RING, 8, TILE), F32),
            dma((CHIPS,)), dma((CHIPS,)), dma((CHIPS,)), dma((CHIPS,)), dma((CHIPS,)), dma((CHIPS,)),
            dma((RING,)), dma((RING,)), dma((RING,)), dma((RING,)), dma((2,)), dma((2,)),
        ],
        compiler_params=pltpu.CompilerParams(
            collective_id=2, has_side_effects=True, vmem_limit_bytes=32 * 2**20),
        name="histograms",
    )(lambdas_again, leaves.reshape(1, OWN), bins_t)
    leaf_values, score_step, histograms = pl.pallas_call(
        finish_kernel,
        out_shape=(
            shape((8, TILE), F32),
            shape((1, OWN), F32),
            shape((3, BINS), F32),
        ),
        in_specs=[VMEM] * 3,
        out_specs=(HBM, HBM, HBM),
        scratch_shapes=[pltpu.VMEM((3, BINS), F32), dma((3,))],
        compiler_params=pltpu.CompilerParams(vmem_limit_bytes=2**21),
        name="finish",
    )(leaf_values, score_step, histograms)
    return lambdas, leaf_values.reshape(LEAVES), score_step.reshape(OWN), histograms


def solution(mesh):
    in_specs = (
        P(("query", "feat")),
        P("query"),
        P(("query", "feat")),
        P(("query", "feat"), None),
        P("query", None),
        P(),
    )
    out_specs = (P(None, ("query", "feat")), P(), P(("query", "feat")), P(None, ("query", "feat")))
    return jax.shard_map(local, mesh=mesh, in_specs=in_specs, out_specs=out_specs, check_vma=False)
```

time: 58.5 us -> 45.1 us (0.77); the launches traced: 57.7 us -> 44.9 us
  Pallas kernels: 51.9 us -> 34.4 us
  starting transfers between devices: 0 us -> 6.57 us
  local copies, waits for them, and re-layouts: 5.14 us -> 3.32 us
    pallas_call x1, Pallas kernels: 33.9 us -> 25.5 us  [local(): pl.pallas_call(histogram_kernel, out_shape=(shape((8, TILE), F32), shape(...]
    ppermute x0 -> x2, starting transfers between devices: none -> 6.57 us  [the longest x1 4.03 us: local(): lax.ppermute(scores, 'feat', [(there, here) for here, there in ring])]
    pallas_call x1, Pallas kernels: 8.17 us -> 2.18 us  [local(): pl.pallas_call(prepare_kernel, out_shape=(shape((8, WIN), F32), shape((8,...]
    pallas_call x1 -> x2, Pallas kernels: 9.8 us -> 6.69 us  [the longest x1 6.06 us: local(): pl.pallas_call(pair_kernel, out_shape=(shape((2, OWN), F32), shape((2, OW...]
    unnamed x17 -> x12, local copies, waits for them, and re-layouts: 5.14 us -> 3.32 us
  transfers between devices with their start and end apart: 0 -> 2, of which waited for: 0 -> 0; matrix products, arithmetic and copies ran while one was open for 0% -> 0% of each run, Pallas kernels for 0% -> 5%
where the time goes in v2:
time: 45.1 us; the launch traced here: 44.9 us
  Pallas kernels  34.4 us (76%)
  starting transfers between devices  6.57 us (15%)
  local copies, waits for them, and re-layouts  3.32 us (7%)
  between operations  0.68 us (2%)
    pallas_call x1, Pallas kernels, local(): pl.pallas_call(histogram_kernel, out_shape=(shape((8, TILE), F32), shape(...  25.5 us
    pallas_call x1, Pallas kernels, local(): pl.pallas_call(pair_kernel, out_shape=(shape((2, OWN), F32), shape((2, OW...  6.06 us
    ppermute x1, starting transfers between devices, local(): lax.ppermute(scores, 'feat', [(there, here) for here, there in ring])  4.03 us
    unnamed x12, local copies, waits for them, and re-layouts  3.32 us
    ppermute x1, starting transfers between devices, local(): from_left = lax.ppermute(scores, 'feat', ring)  2.54 us
    pallas_call x1, Pallas kernels, local(): pl.pallas_call(prepare_kernel, out_shape=(shape((8, WIN), F32), shape((8,...  2.18 us
  transfers between devices with their start and end apart: 2, of which 0 were waited for; matrix products, arithmetic and copies ran while one was open for 0% of the time, Pallas kernels for 5%

profile of v2, /device:TPU:1, one launch (start us, length us, event | category | flops | bytes accessed | tf_op | source)
XLA Modules:
  0.0 44.9 jit_solution(1053517089757255336)
XLA Ops:
  0.6 2.5 %collective-permute-start = (f32[1024]{0:T(1024)}, f32[1024]{0:T(1024)S(1)}, u32[]{:S(2)}, u32[]{:S(2)}) collective-permute-start(f32[1024]{0:T(1024)} %param.6), channel_id=1, source_target_pairs={{0,1},{1,2},{2,3},{3,4},{4,5},{5,6},{6,7},{7,0},{8,9},{9,10},{10,1... | collective-permute-start | bytes 12296 | tf_op jit(solution)/shard_map/ppermute | solution.py:527
  3.2 4.0 %collective-permute-start.1 = (f32[1024]{0:T(1024)}, f32[1024]{0:T(1024)S(1)}, u32[]{:S(2)}, u32[]{:S(2)}) collective-permute-start(f32[1024]{0:T(1024)} %param.6), channel_id=1, source_target_pairs={{1,0},{2,1},{3,2},{4,3},{5,4},{6,5},{7,6},{0,7},{9,8},{10,9},{11,1... | collective-permute-start | bytes 12296 | tf_op jit(solution)/shard_map/ppermute | solution.py:528
  7.2 0.0 copy-start.2
  7.2 1.2 %copy-done.2 = s32[1024,256]{1,0:T(8,128)S(1)} copy-done((s32[1024,256]{1,0:T(8,128)S(1)}, s32[1024,256]{1,0:T(8,128)}, u32[]{:S(2)}) %copy-start.2) | copy-done | bytes 1048600
  8.4 0.0 copy-start.3
  8.4 0.8 %copy-done.3 = s32[8192]{0:T(1024)S(1)} copy-done((s32[8192]{0:T(1024)S(1)}, s32[8192]{0:T(1024)}, u32[]{:S(2)}) %copy-start.3) | copy-done | bytes 32792
  9.2 0.0 copy-start.4
  9.2 0.7 %copy-done.4 = s32[256]{0:T(256)S(1)} copy-done((s32[256]{0:T(256)S(1)}, s32[256]{0:T(256)}, u32[]{:S(2)}) %copy-start.4) | copy-done | bytes 1048
  9.9 0.0 copy-start.5
  9.9 0.7 %copy-done.5 = s32[1,32]{1,0:T(1,128)S(1)} copy-done((s32[1,32]{1,0:T(1,128)S(1)}, s32[1,32]{1,0:T(1,128)}, u32[]{:S(2)}) %copy-start.5) | copy-done | bytes 152
  10.5 0.0 copy-start
  10.5 2.2 %prepare.1 = (f32[8,3072]{1,0:T(8,128)S(1)}, s32[8,128]{1,0:T(8,128)S(1)}, f32[256,1024]{1,0:T(8,128)S(1)}, f32[3072,128]{1,0:T(8,128)S(1)}, f32[3072,128]{1,0:T(8,128)S(1)}) custom-call(s32[1,8192]{1,0:T(1,128)S(1)} %bitcast.12, s32[1,32]{1,0:T(1,128)S(1)} %copy-done.5, s32[1,256]{1,0:T(1,128)S(1)} %bitcast.13, s32[1024,256]{1,0:T(8,128)S(1)} %copy-done.2), custom_call_target="tpu_custom_call" | custom-call | flops 1073741824 | bytes 8388608 | tf_op jit(solution)/shard_map/prepare/pallas_call | solution.py:529
  12.7 0.0 collective-permute-done
  12.7 0.0 collective-permute-done.1
  12.7 0.0 copy-done
  12.7 0.0 copy-start.1
  12.8 6.1 %pairs.1 = (f32[2,1024]{1,0:T(2,128)}, f32[2,1024]{1,0:T(2,128)S(1)}) custom-call(s32[8,128]{1,0:T(8,128)S(1)} %get-tuple-element.17.table, f32[1,1024]{1,0:T(1,128)S(1)} %bitcast.10, f32[1,1024]{1,0:T(1,128)S(1)} %bitcast.8, f32[1,1024]{1,0:T(1,128)S(1)} %bitcast.11, f32[8,3072]{1,0:T(8,128)S(1)} %get-tuple-element.18.rows, ...), custom_call_target="tpu_custom_call" | custom-call | tf_op jit(solution)/shard_map/pairs/pallas_call | solution.py:544
  18.8 0.0 copy-done.1
  18.8 25.5 %histograms.1 = (f32[8,128]{1,0:T(8,128)S(1)}, f32[1,1024]{1,0:T(1,128)S(1)}, f32[8,128]{1,0:T(8,128)S(1)}) custom-call(f32[2,1024]{1,0:T(2,128)S(1)} %get-tuple-element.22.lambdas, s32[1,1024]{1,0:T(1,128)S(1)} %bitcast.9, f32[256,1024]{1,0:T(8,128)S(1)} %get-tuple-element.23.bins_t), custom_call_target="tpu_custom_call" | custom-call | tf_op jit(solution)/shard_map/histograms/pallas_call | solution.py:554
  44.3 0.6 %finish.1 = (f32[8,128]{1,0:T(8,128)}, f32[1,1024]{1,0:T(1,128)}, f32[3,256]{1,0:T(4,128)}) custom-call(f32[8,128]{1,0:T(8,128)S(1)} %get-tuple-element.24.leaf_in, f32[1,1024]{1,0:T(1,128)S(1)} %get-tuple-element.25.step_in, f32[8,128]{1,0:T(8,128)S(1)} %get-tuple-element.26.hist_in), custom_call_target="tpu_custom_call" | custom-call | tf_op jit(solution)/shard_map/finish/pallas_call | solution.py:582
Async XLA Ops:
  0.6 12.1 %collective-permute-start = (f32[1024]{0:T(1024)}, f32[1024]{0:T(1024)S(1)}, u32[]{:S(2)}, u32[]{:S(2)}) collective-permute-start(f32[1024]{0:T(1024)} %param.6), channel_id=1, source_target_pairs={{0,1},{1,2},{2,3},{3,4},{4,5},{5,6},{6,7},{7,0},{8,9},{9,10},{10,1... | collective-permute-start | bytes 12296 | tf_op jit(solution)/shard_map/ppermute | solution.py:527
  3.2 9.5 %collective-permute-start.1 = (f32[1024]{0:T(1024)}, f32[1024]{0:T(1024)S(1)}, u32[]{:S(2)}, u32[]{:S(2)}) collective-permute-start(f32[1024]{0:T(1024)} %param.6), channel_id=1, source_target_pairs={{1,0},{2,1},{3,2},{4,3},{5,4},{6,5},{7,6},{0,7},{9,8},{10,9},{11,1... | collective-permute-start | bytes 12296 | tf_op jit(solution)/shard_map/ppermute | solution.py:528
  7.2 1.2 %copy-start.2 = (s32[1024,256]{1,0:T(8,128)S(1)}, s32[1024,256]{1,0:T(8,128)}, u32[]{:S(2)}) copy-start(s32[1024,256]{1,0:T(8,128)} %bins.1) | copy-start | bytes 3145732
  8.4 0.8 %copy-start.3 = (s32[8192]{0:T(1024)S(1)}, s32[8192]{0:T(1024)}, u32[]{:S(2)}) copy-start(s32[8192]{0:T(1024)} %param.7) | copy-start | bytes 98308
  9.2 0.7 %copy-start.4 = (s32[256]{0:T(256)S(1)}, s32[256]{0:T(256)}, u32[]{:S(2)}) copy-start(s32[256]{0:T(256)} %param.11) | copy-start | bytes 3076
  9.9 0.7 %copy-start.5 = (s32[1,32]{1,0:T(1,128)S(1)}, s32[1,32]{1,0:T(1,128)}, u32[]{:S(2)}) copy-start(s32[1,32]{1,0:T(1,128)} %lengths.1) | copy-start | bytes 388
  10.5 2.2 %copy-start = (f32[1024]{0:T(1024)S(1)}, f32[1024]{0:T(1024)}, u32[]{:S(2)}) copy-start(f32[1024]{0:T(1024)} %param.6) | copy-start | bytes 12292
  12.7 6.1 %copy-start.1 = (s32[1024]{0:T(1024)S(1)}, s32[1024]{0:T(1024)}, u32[]{:S(2)}) copy-start(s32[1024]{0:T(1024)} %param.8) | copy-start | bytes 12292

commit v3 on v2

--- a/solution.py
+++ b/solution.py
@@ -15,7 +15,7 @@
 TILE = 128
 TILES = WIN // TILE
 OWN_TILES = OWN // TILE
-STEP = 64
+STEP = 128
 PAIR = 2 * TILE
 CHIPS = 16
 SIDE = 4
@@ -41,18 +41,34 @@
     return lax.dot_general(left, right, (((1,), (1,)), ((), ())), preferred_element_type=F32)
 
 
+def spread(line):
+    return jnp.broadcast_to(line, (TILE, TILE)).T
+
+
+def in_hbm(array):
+    return pltpu.with_memory_space_constraint(array, pltpu.HBM)
+
+
 def iota(shape, axis):
     return lax.broadcasted_iota(jnp.int32, shape, axis)
 
 
-def prepare_kernel(labels, lengths, owner, bins, rows, table, bins_t, id_col, worth_col):
+def prepare_kernel(
+    labels_in, lengths_in, owner_in, bins_in, rows, table, bins_t, id_col, worth_col,
+    labels, lengths, owner, bins, load_sem
+):
     feat = lax.axis_index("feat")
     left = lax.rem(feat + RING - 1, RING)
     right = lax.rem(feat + 1, RING)
 
-    pick_t = (iota((FEATURES, FEATURES), 0) == owner[...]).astype(F32)
-    pick = pick_t.T.astype(BF16)
-    bins_t[...] = nt_dot(pick, bins[...].astype(F32).astype(BF16))
+    loads = [
+        pltpu.make_async_copy(source, target, load_sem.at[which])
+        for which, (source, target) in enumerate((
+            (lengths_in, lengths), (labels_in, labels), (owner_in, owner), (bins_in, bins)))]
+    for load in loads:
+        load.start()
+    for load in loads[:2]:
+        load.wait()
 
     base = (feat * OWN - OWN).astype(F32)
     length_row = jnp.broadcast_to(lengths[...].astype(F32), (QUERIES, QUERIES))
@@ -97,28 +113,28 @@
     table[...] = (bounds - base).astype(jnp.int32)
 
     rows[...] = jnp.concatenate([ids, worth, own_inverse, own_inverse] * 2, axis=0)
-    pair_lines = jnp.concatenate([ids, worth] * 4, axis=0)
     for tile in range(TILES):
         at = slice(tile * TILE, (tile + 1) * TILE)
-        flipped = pair_lines[:, at].T
-        id_col[at, :] = jnp.broadcast_to(flipped[:, 0:1], (TILE, TILE))
-        worth_col[at, :] = jnp.broadcast_to(flipped[:, 1:2], (TILE, TILE))
+        id_col[at, :] = spread(ids[:, at])
+        worth_col[at, :] = spread(worth[:, at])
+
+    for load in loads[2:]:
+        load.wait()
+    pick_t = (iota((FEATURES, FEATURES), 0) == owner[...]).astype(F32)
+    pick = pick_t.T.astype(BF16)
+    bins_t[...] = nt_dot(pick, bins[...].astype(F32).astype(BF16))
 
 
 def pair_kernel(
     table, from_left, scores, from_right, rows, id_col, worth_col, out, out_again,
     lines, score_col, up_col, discount_col, counts, discount_row, grads, curvs
 ):
-    def spread(column):
-        return jnp.broadcast_to(column, (TILE, TILE))
-
     window = jnp.concatenate([from_left[...], scores[...], from_right[...]], axis=1)
     lines[...] = jnp.concatenate([window, jnp.exp(-window), jnp.exp(window), window] * 2, axis=0)
     for tile in range(TILES):
         at = slice(tile * TILE, (tile + 1) * TILE)
-        flipped = lines[:, at].T
-        score_col[at, :] = spread(flipped[:, 0:1])
-        up_col[at, :] = spread(flipped[:, 1:2])
+        score_col[at, :] = spread(lines[0:1, at])
+        up_col[at, :] = spread(lines[1:2, at])
     counts[...] = jnp.zeros_like(counts)
 
     active = table[2, 0] // PAIR
@@ -174,7 +190,7 @@
     discount_row[...] = discount
     for tile in range(TILES):
         at = slice(tile * TILE, (tile + 1) * TILE)
-        discount_col[at, :] = spread(discount[:, at].T[:, 0:1])
+        discount_col[at, :] = spread(discount[0:1, at])
 
     def own_pair(index, carry):
         pair = index + OWN // PAIR
@@ -250,8 +266,17 @@
     sibling = chip * 2 + other_core
     chip_y, chip_x = lax.div(chip, SIDE), lax.rem(chip, SIDE)
 
+    def steps_to(offset):
+        turn = lax.rem(offset + CHIPS - 1, CHIPS)
+        return lax.rem(lax.div(turn, SIDE) + 1, SIDE), lax.rem(lax.rem(turn, SIDE) + 1, SIDE)
+
     def chip_peer(offset):
-        return lax.rem(chip_y + lax.div(offset, SIDE), SIDE) * SIDE + lax.rem(chip_x + lax.rem(offset, SIDE), SIDE)
+        down, across = steps_to(offset)
+        return lax.rem(chip_y + down, SIDE) * SIDE + lax.rem(chip_x + across, SIDE)
+
+    def chip_source(offset):
+        down, across = steps_to(offset)
+        return lax.rem(chip_y + SIDE - down, SIDE) * SIDE + lax.rem(chip_x + SIDE - across, SIDE)
 
     def ring_peer(offset):
         return lax.rem(feat + offset, RING)
@@ -277,11 +302,11 @@
     leaf_lane = jnp.bitwise_and(leaf, 127)
     in_row = iota((8, OWN), 0) == leaf_row
     lane_hot = (iota((TILE, OWN), 0) == leaf_lane).astype(F32).astype(BF16)
-    spread = []
+    placed = []
     for value in (grad, curv):
         for piece in in_pieces(value, 3):
-            spread.append(jnp.where(in_row, piece.astype(F32), 0.0).astype(BF16))
-    leaf_sums = nt_dot(jnp.concatenate(spread, axis=0), lane_hot)
+            placed.append(jnp.where(in_row, piece.astype(F32), 0.0).astype(BF16))
+    leaf_sums = nt_dot(jnp.concatenate(placed, axis=0), lane_hot)
     leaf_mine[0] = leaf_sums[0:8] + leaf_sums[8:16] + leaf_sums[16:24]
     leaf_mine[1] = leaf_sums[24:32] + leaf_sums[32:40] + leaf_sums[40:48]
     chunk[...] = jnp.zeros_like(chunk)
@@ -348,7 +373,7 @@
         return remote(sent.at[peer], got.at[chip], send_sem.at[peer], recv_sem.at[chip], (peer * 2 + core, feat))
 
     def plane_arrival(offset):
-        peer = chip_peer(offset)
+        peer = chip_source(offset)
         return remote(sent.at[peer], got.at[peer], send_sem.at[peer], recv_sem.at[peer], (peer * 2 + core, feat))
 
     def join(turn):
@@ -426,7 +451,7 @@
 
     def add_hist(offset, total):
         plane_arrival(offset).wait_recv()
-        return total + got[chip_peer(offset)]
+        return total + got[chip_source(offset)]
 
     summed = lax.fori_loop(1, CHIPS, add_hist, sent[chip])
 
@@ -535,12 +560,15 @@
             shape((WIN, TILE), F32),
             shape((WIN, TILE), F32),
         ),
-        in_specs=[VMEM] * 4,
+        in_specs=[HBM] * 4,
         out_specs=(VMEM,) * 5,
+        scratch_shapes=[
+            pltpu.VMEM((1, BLOCK), jnp.int32), pltpu.VMEM((1, QUERIES), jnp.int32),
+            pltpu.VMEM((1, FEATURES), jnp.int32), pltpu.VMEM((OWN, FEATURES), jnp.int32), dma((4,))],
         cost_estimate=pl.CostEstimate(flops=2**30, bytes_accessed=2**23, transcendentals=0),
         compiler_params=pltpu.CompilerParams(vmem_limit_bytes=32 * 2**20),
         name="prepare",
-    )(labels.reshape(1, BLOCK), lengths, owner.reshape(1, FEATURES), bins)
+    )(in_hbm(labels.reshape(1, BLOCK)), in_hbm(lengths), in_hbm(owner.reshape(1, FEATURES)), in_hbm(bins))
     lambdas, lambdas_again = pl.pallas_call(
         pair_kernel,
         out_shape=(shape((2, OWN), F32), shape((2, OWN), F32)),

time: 45.1 us -> 41.6 us (0.922)
  local copies, waits for them, and re-layouts: 3.32 us -> 0.01 us
    unnamed x12 -> x4, local copies, waits for them, and re-layouts: 3.32 us -> 0.01 us
    pallas_call x1, Pallas kernels: 25.5 us -> 25 us  [local(): pl.pallas_call(histogram_kernel, out_shape=(shape((8, TILE), F32), shape(...]
  transfers between devices with their start and end apart: 2 -> 2, of which waited for: 0 -> 0; matrix products, arithmetic and copies ran while one was open for 0% -> 0% of each run, Pallas kernels for 5% -> 6%
where the time goes in v3:
time: 41.6 us; the launch traced here: 41.5 us
  Pallas kernels  34.3 us (82%)
  starting transfers between devices  6.57 us (16%)
  between operations  0.68 us (2%)
    pallas_call x1, Pallas kernels, local(): pl.pallas_call(histogram_kernel, out_shape=(shape((8, TILE), F32), shape(...  25 us
    pallas_call x1, Pallas kernels, local(): pl.pallas_call(pair_kernel, out_shape=(shape((2, OWN), F32), shape((2, OW...  6.31 us
    ppermute x1, starting transfers between devices, local(): lax.ppermute(scores, 'feat', [(there, here) for here, there in ring])  4.03 us
    ppermute x1, starting transfers between devices, local(): from_left = lax.ppermute(scores, 'feat', ring)  2.54 us
    pallas_call x1, Pallas kernels, local(): pl.pallas_call(prepare_kernel, out_shape=(shape((8, WIN), F32), shape((8,...  2.34 us
  transfers between devices with their start and end apart: 2, of which 0 were waited for; matrix products, arithmetic and copies ran while one was open for 0% of the time, Pallas kernels for 6%

profile of v3, /device:TPU:1, one launch (start us, length us, event | category | flops | bytes accessed | tf_op | source)
XLA Modules:
  0.0 41.5 jit_solution(10000682604572064700)
XLA Ops:
  0.6 2.5 %collective-permute-start = (f32[1024]{0:T(1024)}, f32[1024]{0:T(1024)S(1)}, u32[]{:S(2)}, u32[]{:S(2)}) collective-permute-start(f32[1024]{0:T(1024)} %param.6), channel_id=1, source_target_pairs={{0,1},{1,2},{2,3},{3,4},{4,5},{5,6},{6,7},{7,0},{8,9},{9,10},{10,1... | collective-permute-start | bytes 12296 | tf_op jit(solution)/shard_map/ppermute | solution.py:552
  3.2 4.0 %collective-permute-start.1 = (f32[1024]{0:T(1024)}, f32[1024]{0:T(1024)S(1)}, u32[]{:S(2)}, u32[]{:S(2)}) collective-permute-start(f32[1024]{0:T(1024)} %param.6), channel_id=1, source_target_pairs={{1,0},{2,1},{3,2},{4,3},{5,4},{6,5},{7,6},{0,7},{9,8},{10,9},{11,1... | collective-permute-start | bytes 12296 | tf_op jit(solution)/shard_map/ppermute | solution.py:553
  7.2 0.0 copy-start
  7.2 2.3 %prepare.1 = (f32[8,3072]{1,0:T(8,128)S(1)}, s32[8,128]{1,0:T(8,128)S(1)}, f32[256,1024]{1,0:T(8,128)S(1)}, f32[3072,128]{1,0:T(8,128)S(1)}, f32[3072,128]{1,0:T(8,128)S(1)}) custom-call(s32[1,8192]{1,0:T(1,128)} %bitcast.12, s32[1,32]{1,0:T(1,128)} %lengths_in.1, s32[1,256]{1,0:T(1,128)} %bitcast.15, s32[1024,256]{1,0:T(8,128)} %bins_in.1), custom_call_target="tpu_custom_call" | custom-call | flops 1073741824 | bytes 8388608 | tf_op jit(solution)/shard_map/prepare/pallas_call | solution.py:554
  9.5 0.0 collective-permute-done
  9.6 0.0 collective-permute-done.1
  9.6 0.0 copy-done
  9.6 0.0 copy-start.1
  9.6 6.3 %pairs.1 = (f32[2,1024]{1,0:T(2,128)}, f32[2,1024]{1,0:T(2,128)S(1)}) custom-call(s32[8,128]{1,0:T(8,128)S(1)} %get-tuple-element.17.table, f32[1,1024]{1,0:T(1,128)S(1)} %bitcast.10, f32[1,1024]{1,0:T(1,128)S(1)} %bitcast.8, f32[1,1024]{1,0:T(1,128)S(1)} %bitcast.11, f32[8,3072]{1,0:T(8,128)S(1)} %get-tuple-element.18.rows, ...), custom_call_target="tpu_custom_call" | custom-call | tf_op jit(solution)/shard_map/pairs/pallas_call | solution.py:572
  15.9 0.0 copy-done.1
  15.9 25.0 %histograms.1 = (f32[8,128]{1,0:T(8,128)S(1)}, f32[1,1024]{1,0:T(1,128)S(1)}, f32[8,128]{1,0:T(8,128)S(1)}) custom-call(f32[2,1024]{1,0:T(2,128)S(1)} %get-tuple-element.22.lambdas, s32[1,1024]{1,0:T(1,128)S(1)} %bitcast.9, f32[256,1024]{1,0:T(8,128)S(1)} %get-tuple-element.23.bins_t), custom_call_target="tpu_custom_call" | custom-call | tf_op jit(solution)/shard_map/histograms/pallas_call | solution.py:582
  40.9 0.6 %finish.1 = (f32[8,128]{1,0:T(8,128)}, f32[1,1024]{1,0:T(1,128)}, f32[3,256]{1,0:T(4,128)}) custom-call(f32[8,128]{1,0:T(8,128)S(1)} %get-tuple-element.24.leaf_in, f32[1,1024]{1,0:T(1,128)S(1)} %get-tuple-element.25.step_in, f32[8,128]{1,0:T(8,128)S(1)} %get-tuple-element.26.hist_in), custom_call_target="tpu_custom_call" | custom-call | tf_op jit(solution)/shard_map/finish/pallas_call | solution.py:610
Async XLA Ops:
  0.6 8.9 %collective-permute-start = (f32[1024]{0:T(1024)}, f32[1024]{0:T(1024)S(1)}, u32[]{:S(2)}, u32[]{:S(2)}) collective-permute-start(f32[1024]{0:T(1024)} %param.6), channel_id=1, source_target_pairs={{0,1},{1,2},{2,3},{3,4},{4,5},{5,6},{6,7},{7,0},{8,9},{9,10},{10,1... | collective-permute-start | bytes 12296 | tf_op jit(solution)/shard_map/ppermute | solution.py:552
  3.2 6.4 %collective-permute-start.1 = (f32[1024]{0:T(1024)}, f32[1024]{0:T(1024)S(1)}, u32[]{:S(2)}, u32[]{:S(2)}) collective-permute-start(f32[1024]{0:T(1024)} %param.6), channel_id=1, source_target_pairs={{1,0},{2,1},{3,2},{4,3},{5,4},{6,5},{7,6},{0,7},{9,8},{10,9},{11,1... | collective-permute-start | bytes 12296 | tf_op jit(solution)/shard_map/ppermute | solution.py:553
  7.2 2.4 %copy-start = (f32[1024]{0:T(1024)S(1)}, f32[1024]{0:T(1024)}, u32[]{:S(2)}) copy-start(f32[1024]{0:T(1024)} %param.6) | copy-start | bytes 12292
  9.6 6.3 %copy-start.1 = (s32[1024]{0:T(1024)S(1)}, s32[1024]{0:T(1024)}, u32[]{:S(2)}) copy-start(s32[1024]{0:T(1024)} %param.8) | copy-start | bytes 12292

commit v4 on v3

--- a/solution.py
+++ b/solution.py
@@ -21,7 +21,7 @@
 SIDE = 4
 RING = 8
 GROUP = 8
-EARLY = 5
+EARLY = 4
 HI = 8
 LO = 32
 
@@ -54,19 +54,32 @@
 
 
 def prepare_kernel(
-    labels_in, lengths_in, owner_in, bins_in, rows, table, bins_t, id_col, worth_col,
-    labels, lengths, owner, bins, load_sem
+    scores_in, labels_in, lengths_in, owner_in, bins_in, window, rows, table, bins_t, id_col, worth_col,
+    labels, lengths, owner, bins, own_scores, from_left, from_right, load_sem, send_sem, recv_sem
 ):
     feat = lax.axis_index("feat")
+    query = lax.axis_index("query")
     left = lax.rem(feat + RING - 1, RING)
     right = lax.rem(feat + 1, RING)
 
+    barrier = pltpu.get_barrier_semaphore()
+    for peer in (left, right):
+        pl.semaphore_signal(barrier, inc=1, device_id=(query, peer), device_id_type=MESH_ID)
     loads = [
         pltpu.make_async_copy(source, target, load_sem.at[which])
         for which, (source, target) in enumerate((
-            (lengths_in, lengths), (labels_in, labels), (owner_in, owner), (bins_in, bins)))]
+            (lengths_in, lengths), (labels_in, labels), (owner_in, owner), (bins_in, bins), (scores_in, own_scores)))]
     for load in loads:
         load.start()
+    to_right = pltpu.make_async_remote_copy(
+        src_ref=scores_in, dst_ref=from_left, send_sem=send_sem.at[0], recv_sem=recv_sem.at[0],
+        device_id=(query, right), device_id_type=MESH_ID)
+    to_left = pltpu.make_async_remote_copy(
+        src_ref=scores_in, dst_ref=from_right, send_sem=send_sem.at[1], recv_sem=recv_sem.at[1],
+        device_id=(query, left), device_id_type=MESH_ID)
+    pl.semaphore_wait(barrier, 2)
+    to_right.start()
+    to_left.start()
     for load in loads[:2]:
         load.wait()
 
@@ -124,12 +137,18 @@
     pick = pick_t.T.astype(BF16)
     bins_t[...] = nt_dot(pick, bins[...].astype(F32).astype(BF16))
 
+    window[:, OWN:2 * OWN] = own_scores[...]
+    to_right.wait()
+    to_left.wait()
+    window[:, 0:OWN] = from_left[...]
+    window[:, 2 * OWN:WIN] = from_right[...]
+
 
 def pair_kernel(
-    table, from_left, scores, from_right, rows, id_col, worth_col, out, out_again,
+    table, window_in, rows, id_col, worth_col, out, out_again,
     lines, score_col, up_col, discount_col, counts, discount_row, grads, curvs
 ):
-    window = jnp.concatenate([from_left[...], scores[...], from_right[...]], axis=1)
+    window = window_in[...]
     lines[...] = jnp.concatenate([window, jnp.exp(-window), jnp.exp(window), window] * 2, axis=0)
     for tile in range(TILES):
         at = slice(tile * TILE, (tile + 1) * TILE)
@@ -254,7 +273,7 @@
 def histogram_kernel(
     lambdas, leaves, bins_t, leaf_out, step_out, hist_out,
     left_side, right_side, weights, pair_sent, pair_got, sent, got,
-    leaf_mine, leaf_pair, leaf_got, leaf_ring, leaf_both, chunk, chunk_got,
+    leaf_got, leaf_ring, leaf_both, chunk, chunk_got,
     pair_send, pair_recv, send_sem, recv_sem, leaf_send, leaf_recv, ring_send, ring_recv,
     chunk_send, chunk_recv, one_send, one_recv
 ):
@@ -307,8 +326,8 @@
         for piece in in_pieces(value, 3):
             placed.append(jnp.where(in_row, piece.astype(F32), 0.0).astype(BF16))
     leaf_sums = nt_dot(jnp.concatenate(placed, axis=0), lane_hot)
-    leaf_mine[0] = leaf_sums[0:8] + leaf_sums[8:16] + leaf_sums[16:24]
-    leaf_mine[1] = leaf_sums[24:32] + leaf_sums[32:40] + leaf_sums[40:48]
+    leaf_got[chip, 0:8, :] = leaf_sums[0:8] + leaf_sums[8:16] + leaf_sums[16:24]
+    leaf_got[chip, 8:16, :] = leaf_sums[24:32] + leaf_sums[32:40] + leaf_sums[40:48]
     chunk[...] = jnp.zeros_like(chunk)
 
     stats = in_pieces(grad, 2) + in_pieces(curv, 2) + [jnp.ones((1, OWN), BF16)]
@@ -357,12 +376,14 @@
     def chip_at(turn):
         return chip_peer(lax.rem(turn + 1, CHIPS))
 
-    def both_groups(turn):
-        peer = chip_at(turn)
-        one_hots(peer * 2 + other_core, 0)
-        one_hots(peer * 2 + core, 1)
-        sums(0, pair_sent, peer)
-        sums(1, sent, peer)
+    def groups_of(turns):
+        peers = [chip_at(turn) for turn in turns]
+        for which, peer in enumerate(peers):
+            one_hots(peer * 2 + other_core, 2 * which)
+            one_hots(peer * 2 + core, 2 * which + 1)
+        for which, peer in enumerate(peers):
+            sums(2 * which, pair_sent, peer)
+            sums(2 * which + 1, sent, peer)
 
     def pair_copy(turn):
         peer = chip_at(turn)
@@ -381,61 +402,63 @@
         peer = chip_at(turn)
         sent[peer] = sent[peer] + pair_got[peer]
 
-    @pl.loop(0, EARLY)
-    def _(turn):
-        both_groups(turn)
+    def join_and_send(turn):
+        join(turn)
+        plane_copy(turn + 1).start()
+
+    @pl.loop(0, EARLY // 2)
+    def _(step):
+        groups_of((2 * step, 2 * step + 1))
 
     pl.semaphore_wait(barrier, 1 + CHIPS - 1 + RING - 1)
 
-    leaf_swap = remote(leaf_mine.at[other_core], leaf_pair, one_send.at[0], one_recv.at[0], (sibling, feat))
-    leaf_swap.start()
+    def leaf_copy(offset):
+        peer = chip_peer(offset)
+        return remote(leaf_got.at[chip], leaf_got.at[chip], leaf_send.at[peer], leaf_recv.at[chip], (peer * 2 + core, feat))
+
+    def leaf_arrival(offset):
+        peer = chip_source(offset)
+        return remote(leaf_got.at[chip], leaf_got.at[peer], leaf_send.at[peer], leaf_recv.at[peer], (peer * 2 + core, feat))
+
+    @pl.loop(1, CHIPS)
+    def _(offset):
+        leaf_copy(offset).start()
 
     @pl.loop(0, EARLY)
     def _(turn):
         pair_copy(turn).start()
 
-    both_groups(EARLY)
+    groups_of((EARLY, EARLY + 1))
     pair_copy(EARLY).start()
-    both_groups(EARLY + 1)
     pair_copy(EARLY + 1).start()
 
-    @pl.loop(1, EARLY + 1)
+    @pl.loop(0, EARLY)
     def _(turn):
-        join(turn - 1)
-        plane_copy(turn).start()
-
-    leaf_swap.wait_recv()
-    leaf_got[chip] = leaf_mine[core] + leaf_pair[...]
-
-    def leaf_copy(offset):
-        peer = chip_peer(offset)
-        return remote(leaf_got.at[chip], leaf_got.at[chip], leaf_send.at[peer], leaf_recv.at[chip], (peer * 2 + core, feat))
-
-    def leaf_arrival(offset):
-        peer = chip_peer(offset)
-        return remote(leaf_got.at[chip], leaf_got.at[peer], leaf_send.at[peer], leaf_recv.at[peer], (peer * 2 + core, feat))
+        join_and_send(turn)
+
+    @pl.loop(EARLY // 2 + 1, CHIPS // 2 - 1)
+    def _(step):
+        groups_of((2 * step, 2 * step + 1))
+        pair_copy(2 * step).start()
+        pair_copy(2 * step + 1).start()
+        join_and_send(2 * step - 2)
+        join_and_send(2 * step - 1)
+
+    groups_of((CHIPS - 2,))
+    pair_copy(CHIPS - 2).start()
+    join_and_send(CHIPS - 4)
+    join_and_send(CHIPS - 3)
+    groups_of((CHIPS - 1,))
+    pair_copy(CHIPS - 1).start()
+    join_and_send(CHIPS - 2)
+    join(CHIPS - 1)
 
     @pl.loop(1, CHIPS)
     def _(offset):
-        leaf_copy(offset).start()
-
-    @pl.loop(EARLY + 2, CHIPS)
-    def _(turn):
-        both_groups(turn)
-        pair_copy(turn).start()
-        join(turn - 2)
-        plane_copy(turn - 1).start()
-
-    join(CHIPS - 2)
-    plane_copy(CHIPS - 1).start()
-    join(CHIPS - 1)
-
-    @pl.loop(1, CHIPS)
-    def _(offset):
         leaf_arrival(offset).wait_recv()
 
     leaf_ring[feat] = lax.fori_loop(
-        0, CHIPS, lambda peer, total: total + leaf_got[peer], jnp.zeros((8, TILE), F32))
+        0, CHIPS, lambda peer, total: total + leaf_got[peer], jnp.zeros((16, TILE), F32))
 
     def ring_copy(offset):
         peer = ring_peer(offset)
@@ -489,17 +512,18 @@
     def _(offset):
         ring_arrival(offset).wait_recv()
 
-    half_total = leaf_ring[0]
+    core_total = leaf_ring[0]
     for peer in range(1, RING):
-        half_total = half_total + leaf_ring[peer]
-    leaf_both[core] = half_total
-    leaf_back = remote(leaf_both.at[core], leaf_both.at[core], one_send.at[1], one_recv.at[1], (sibling, feat))
+        core_total = core_total + leaf_ring[peer]
+    leaf_both[core] = core_total
+    leaf_back = remote(leaf_both.at[core], leaf_both.at[core], one_send.at[0], one_recv.at[0], (sibling, feat))
     leaf_back.start()
 
     leaf_back_here = remote(
-        leaf_both.at[core], leaf_both.at[other_core], one_send.at[1], one_recv.at[1], (sibling, feat))
+        leaf_both.at[core], leaf_both.at[other_core], one_send.at[0], one_recv.at[0], (sibling, feat))
     leaf_back_here.wait_recv()
-    total_grad, total_curv = leaf_both[0], leaf_both[1]
+    totals = leaf_both[0] + leaf_both[1]
+    total_grad, total_curv = totals[0:8], totals[8:16]
     shrunk = jnp.maximum(jnp.abs(total_grad) - lasso_penalty, 0.0) / (total_curv + ridge_penalty)
     values = jnp.where(total_grad > 0.0, -shrunk, shrunk)
     leaf_out[...] = values
@@ -514,7 +538,6 @@
 
     hist_out[...] = lax.fori_loop(1, RING, add_chunk, chunk[feat])
 
-    leaf_swap.wait_send()
     leaf_back.wait_send()
     pair_copy(CHIPS - 1).wait_send()
 
@@ -548,36 +571,36 @@
     shape = jax.ShapeDtypeStruct
     dma = pltpu.SemaphoreType.DMA
     column = pltpu.VMEM((WIN, TILE), F32)
-    ring = [(place, (place + 1) % RING) for place in range(RING)]
-    from_left = lax.ppermute(scores, "feat", ring)
-    from_right = lax.ppermute(scores, "feat", [(there, here) for here, there in ring])
-    rows, table, bins_t, id_col, worth_col = pl.pallas_call(
+    window, rows, table, bins_t, id_col, worth_col = pl.pallas_call(
         prepare_kernel,
         out_shape=(
+            shape((1, WIN), F32),
             shape((8, WIN), F32),
             shape((8, TILE), jnp.int32),
             shape((FEATURES, OWN), F32),
             shape((WIN, TILE), F32),
             shape((WIN, TILE), F32),
         ),
-        in_specs=[HBM] * 4,
-        out_specs=(VMEM,) * 5,
+        in_specs=[HBM] * 5,
+        out_specs=(VMEM,) * 6,
         scratch_shapes=[
             pltpu.VMEM((1, BLOCK), jnp.int32), pltpu.VMEM((1, QUERIES), jnp.int32),
-            pltpu.VMEM((1, FEATURES), jnp.int32), pltpu.VMEM((OWN, FEATURES), jnp.int32), dma((4,))],
-        cost_estimate=pl.CostEstimate(flops=2**30, bytes_accessed=2**23, transcendentals=0),
-        compiler_params=pltpu.CompilerParams(vmem_limit_bytes=32 * 2**20),
+            pltpu.VMEM((1, FEATURES), jnp.int32), pltpu.VMEM((OWN, FEATURES), jnp.int32),
+            pltpu.VMEM((1, OWN), F32), pltpu.VMEM((1, OWN), F32), pltpu.VMEM((1, OWN), F32),
+            dma((5,)), dma((2,)), dma((2,))],
+        compiler_params=pltpu.CompilerParams(
+            collective_id=1, has_side_effects=True, vmem_limit_bytes=32 * 2**20),
         name="prepare",
-    )(in_hbm(labels.reshape(1, BLOCK)), in_hbm(lengths), in_hbm(owner.reshape(1, FEATURES)), in_hbm(bins))
+    )(in_hbm(scores.reshape(1, OWN)), in_hbm(labels.reshape(1, BLOCK)), in_hbm(lengths), in_hbm(owner.reshape(1, FEATURES)), in_hbm(bins))
     lambdas, lambdas_again = pl.pallas_call(
         pair_kernel,
         out_shape=(shape((2, OWN), F32), shape((2, OWN), F32)),
-        in_specs=[SMEM] + [VMEM] * 6,
+        in_specs=[SMEM] + [VMEM] * 4,
         out_specs=(VMEM, VMEM),
         scratch_shapes=[pltpu.VMEM((8, WIN), F32)] + [column] * 3 + [pltpu.VMEM((8, WIN), F32)] * 2 + [pltpu.VMEM((8, OWN), F32)] * 2,
         compiler_params=pltpu.CompilerParams(vmem_limit_bytes=32 * 2**20),
         name="pairs",
-    )(table, from_left.reshape(1, OWN), scores.reshape(1, OWN), from_right.reshape(1, OWN), rows, id_col, worth_col)
+    )(table, window, rows, id_col, worth_col)
     part = pltpu.VMEM((CHIPS, 3 * HI, GROUP * LO), F32)
     leaf_values, score_step, histograms = pl.pallas_call(
         histogram_kernel,
@@ -589,19 +612,17 @@
         in_specs=[VMEM] * 3,
         out_specs=(VMEM, VMEM, VMEM),
         scratch_shapes=[
-            pltpu.VMEM((2, 5 * GROUP * HI, OWN), BF16),
-            pltpu.VMEM((2, GROUP * LO, OWN), BF16),
+            pltpu.VMEM((4, 5 * GROUP * HI, OWN), BF16),
+            pltpu.VMEM((4, GROUP * LO, OWN), BF16),
             pltpu.VMEM((5, 16, OWN), BF16),
             part, part, part, part,
-            pltpu.VMEM((2, 8, TILE), F32),
-            pltpu.VMEM((8, TILE), F32),
-            pltpu.VMEM((CHIPS, 8, TILE), F32),
-            pltpu.VMEM((RING, 8, TILE), F32),
-            pltpu.VMEM((2, 8, TILE), F32),
+            pltpu.VMEM((CHIPS, 16, TILE), F32),
+            pltpu.VMEM((RING, 16, TILE), F32),
+            pltpu.VMEM((2, 16, TILE), F32),
             pltpu.VMEM((RING, 8, TILE), F32),
             pltpu.VMEM((RING, 8, TILE), F32),
             dma((CHIPS,)), dma((CHIPS,)), dma((CHIPS,)), dma((CHIPS,)), dma((CHIPS,)), dma((CHIPS,)),
-            dma((RING,)), dma((RING,)), dma((RING,)), dma((RING,)), dma((2,)), dma((2,)),
+            dma((RING,)), dma((RING,)), dma((RING,)), dma((RING,)), dma((1,)), dma((1,)),
         ],
         compiler_params=pltpu.CompilerParams(
             collective_id=2, has_side_effects=True, vmem_limit_bytes=32 * 2**20),

time: 41.6 us -> 40.7 us (0.978)
  starting transfers between devices: 6.57 us -> 0 us
  Pallas kernels: 34.3 us -> 39.9 us
    ppermute x2 -> x0, starting transfers between devices: 6.57 us -> none  [the longest x1 4.03 us: local(): lax.ppermute(scores, 'feat', [(there, here) for here, there in ring])]
    pallas_call x1, Pallas kernels: 2.34 us -> 8.58 us  [local(): pl.pallas_call(prepare_kernel, out_shape=(shape((1, WIN), F32), shape((8,...]
    pallas_call x1, Pallas kernels: 6.31 us -> 5.03 us  [local(): pl.pallas_call(pair_kernel, out_shape=(shape((2, OWN), F32), shape((2, OW...]
    pallas_call x1, Pallas kernels: 25 us -> 25.7 us  [local(): pl.pallas_call(histogram_kernel, out_shape=(shape((8, TILE), F32), shape(...]
  transfers between devices with their start and end apart: 2 -> 0, of which waited for: 0 -> 0; matrix products, arithmetic and copies ran while one was open for 0% -> 0% of each run, Pallas kernels for 6% -> 0%
where the time goes in v4:
time: 40.7 us; the launch traced here: 40.6 us
  Pallas kernels  39.9 us (98%)
  between operations  0.66 us (2%)
    pallas_call x1, Pallas kernels, local(): pl.pallas_call(histogram_kernel, out_shape=(shape((8, TILE), F32), shape(...  25.7 us
    pallas_call x1, Pallas kernels, local(): pl.pallas_call(prepare_kernel, out_shape=(shape((1, WIN), F32), shape((8,...  8.58 us
    pallas_call x1, Pallas kernels, local(): pl.pallas_call(pair_kernel, out_shape=(shape((2, OWN), F32), shape((2, OW...  5.03 us

profile of v4, /device:TPU:1, one launch (start us, length us, event | category | flops | bytes accessed | tf_op | source)
XLA Modules:
  0.0 40.6 jit_solution(6598147256831604054)
XLA Ops:
  0.6 8.6 %prepare.1 = (f32[1,3072]{1,0:T(1,128)S(1)}, f32[8,3072]{1,0:T(8,128)S(1)}, s32[8,128]{1,0:T(8,128)S(1)}, f32[256,1024]{1,0:T(8,128)S(1)}, f32[3072,128]{1,0:T(8,128)S(1)}, /*index=5*/f32[3072,128]{1,0:T(8,128)S(1)}) custom-call(f32[1,1024]{1,0:T(1,128)} %bitcast.8, s32[1,8192]{1,0:T(1,128)} %bitcast.7, s32[1,32]{1,0:T(1,128)} %lengths_in.1, ...), custom_call_target="tpu_custom_call" | custom-call | tf_op jit(solution)/shard_map/prepare/pallas_call | solution.py:574
  9.2 0.0 copy-start
  9.2 5.0 %pairs.1 = (f32[2,1024]{1,0:T(2,128)}, f32[2,1024]{1,0:T(2,128)S(1)}) custom-call(s32[8,128]{1,0:T(8,128)S(1)} %get-tuple-element.18.table, f32[1,3072]{1,0:T(1,128)S(1)} %get-tuple-element.19.window_in, f32[8,3072]{1,0:T(8,128)S(1)} %get-tuple-element.20.rows, f32[3072,128]{1,0:T(8,128)S(1)} %get-tuple-element.21.id_col, ...), custom_call_target="tpu_custom_call" | custom-call | tf_op jit(solution)/shard_map/pairs/pallas_call | solution.py:595
  14.3 0.0 copy-done
  14.3 25.7 %histograms.1 = (f32[8,128]{1,0:T(8,128)S(1)}, f32[1,1024]{1,0:T(1,128)S(1)}, f32[8,128]{1,0:T(8,128)S(1)}) custom-call(f32[2,1024]{1,0:T(2,128)S(1)} %get-tuple-element.24.lambdas, s32[1,1024]{1,0:T(1,128)S(1)} %bitcast.6, f32[256,1024]{1,0:T(8,128)S(1)} %get-tuple-element.25.bins_t), custom_call_target="tpu_custom_call" | custom-call | tf_op jit(solution)/shard_map/histograms/pallas_call | solution.py:605
  40.0 0.6 %finish.1 = (f32[8,128]{1,0:T(8,128)}, f32[1,1024]{1,0:T(1,128)}, f32[3,256]{1,0:T(4,128)}) custom-call(f32[8,128]{1,0:T(8,128)S(1)} %get-tuple-element.26.leaf_in, f32[1,1024]{1,0:T(1,128)S(1)} %get-tuple-element.27.step_in, f32[8,128]{1,0:T(8,128)S(1)} %get-tuple-element.28.hist_in), custom_call_target="tpu_custom_call" | custom-call | tf_op jit(solution)/shard_map/finish/pallas_call | solution.py:631
Async XLA Ops:
  9.2 5.0 %copy-start = (s32[1024]{0:T(1024)S(1)}, s32[1024]{0:T(1024)}, u32[]{:S(2)}) copy-start(s32[1024]{0:T(1024)} %param.8) | copy-start | bytes 12292

commit v5 on v4

--- a/solution.py
+++ b/solution.py
@@ -1,3 +1,5 @@
+import functools
+
 import jax
 import jax.numpy as jnp
 from jax import lax
@@ -156,6 +158,11 @@
         up_col[at, :] = spread(lines[1:2, at])
     counts[...] = jnp.zeros_like(counts)
 
+    def blocks_of(pair):
+        low, high = table[0, 2 * pair], table[1, 2 * pair + 1]
+        alone = (low == table[0, 2 * pair + 1]) & (high == table[1, 2 * pair])
+        return low // STEP, (high + STEP - 1) // STEP, (low + STEP - 1) // STEP, high // STEP, alone
+
     active = table[2, 0] // PAIR
     stop = (table[3, 0] + PAIR - 1) // PAIR
 
@@ -164,15 +171,17 @@
         score = jnp.broadcast_to(lines[0:1, pl.ds(begin, PAIR)], (8, PAIR))
         ident = jnp.broadcast_to(rows[0:1, pl.ds(begin, PAIR)], (8, PAIR))
 
-        def count(start, steps, beats, total):
+        def count(start, steps, beats, total, masked=True):
             for sub in range(steps):
                 spot = pl.multiple_of(start + sub * 8, 8)
                 other = score_col[pl.ds(spot, 8), :]
-                other_id = id_col[pl.ds(spot, 8), :]
+                other_id = id_col[pl.ds(spot, 8), :] if masked else None
                 parts = []
                 for half in range(2):
                     lanes = slice(half * TILE, (half + 1) * TILE)
-                    hit = (other_id == ident[:, lanes]) & beats(other, score[:, lanes], half, sub)
+                    hit = beats(other, score[:, lanes], half, sub)
+                    if masked:
+                        hit = hit & (other_id == ident[:, lanes])
                     parts.append(total[half] + jnp.where(hit, 1.0, 0.0))
                 total = tuple(parts)
             return total
@@ -193,12 +202,18 @@
 
         empty = jnp.zeros((8, TILE), F32)
         total = count(begin, PAIR // 8, around, (empty, empty))
-        total = lax.fori_loop(
-            table[0, 2 * pair] // STEP, begin // STEP,
-            lambda i, t: count(i * STEP, STEP // 8, ahead, t), total)
-        total = lax.fori_loop(
-            (begin + PAIR) // STEP, (table[1, 2 * pair + 1] + STEP - 1) // STEP,
-            lambda i, t: count(i * STEP, STEP // 8, behind, t), total)
+        def run(first, stop, beats, masked, total):
+            return lax.fori_loop(
+                first, stop, lambda i, t: count(i * STEP, STEP // 8, beats, t, masked), total)
+
+        low, high, inner_low, inner_high, alone = blocks_of(pair)
+        here, after = begin // STEP, (begin + PAIR) // STEP
+        inner_low = jnp.where(alone, jnp.minimum(inner_low, here), here)
+        inner_high = jnp.where(alone, jnp.maximum(inner_high, after), after)
+        total = run(low, inner_low, ahead, True, total)
+        total = run(inner_low, here, ahead, False, total)
+        total = run(after, inner_high, behind, False, total)
+        total = run(inner_high, high, behind, True, total)
         counts[:, pl.ds(begin, PAIR)] = jnp.concatenate(total, axis=1)
         return carry
 
@@ -223,7 +238,7 @@
         worth = own(rows, 1)
         discount = discount_row[:, pl.ds(begin, PAIR)]
 
-        def meet(block, sums):
+        def meet(masked, block, sums):
             for sub in range(STEP // 8):
                 at = pl.ds(pl.multiple_of(block * STEP + sub * 8, 8), 8)
                 other_up, other_id = up_col[at, :], id_col[at, :]
@@ -234,7 +249,9 @@
                     odds = up[:, lanes] * other_up
                     win = pltpu.reciprocal(1.0 - odds, approx=True)
                     lose = odds * win
-                    gap = jnp.where(other_id == ident[:, lanes], discount[:, lanes] - other_discount, 0.0)
+                    gap = discount[:, lanes] - other_discount
+                    if masked:
+                        gap = jnp.where(other_id == ident[:, lanes], gap, 0.0)
                     rise = worth[:, lanes] - other_worth
                     change = jnp.abs(rise * gap)
                     parts.append(sums[half][0] + change * jnp.where(rise > 0.0, win, lose))
@@ -243,9 +260,12 @@
             return sums
 
         empty = jnp.zeros((8, TILE), F32)
-        sums = lax.fori_loop(
-            table[0, 2 * pair] // STEP, (table[1, 2 * pair + 1] + STEP - 1) // STEP, meet,
-            ((empty, empty), (empty, empty)))
+        low, high, inner_low, inner_high, alone = blocks_of(pair)
+        inner_low = jnp.where(alone, inner_low, high)
+        inner_high = jnp.where(alone, inner_high, high)
+        sums = ((empty, empty), (empty, empty))
+        for first, stop, masked in ((low, inner_low, True), (inner_low, inner_high, False), (inner_high, high, True)):
+            sums = lax.fori_loop(first, stop, functools.partial(meet, masked), sums)
         for half in range(2):
             spot = pl.ds(pl.multiple_of(index * PAIR + half * TILE, TILE), TILE)
             grads[:, spot] = sums[half][0]
@@ -450,9 +470,6 @@
     join_and_send(CHIPS - 3)
     groups_of((CHIPS - 1,))
     pair_copy(CHIPS - 1).start()
-    join_and_send(CHIPS - 2)
-    join(CHIPS - 1)
-
     @pl.loop(1, CHIPS)
     def _(offset):
         leaf_arrival(offset).wait_recv()
@@ -471,6 +488,9 @@
     @pl.loop(1, RING)
     def _(offset):
         ring_copy(offset).start()
+
+    join_and_send(CHIPS - 2)
+    join(CHIPS - 1)
 
     def add_hist(offset, total):
         plane_arrival(offset).wait_recv()

time: 40.7 us -> 40.9 us (level)
    pallas_call x1, Pallas kernels: 5.03 us -> 5.5 us  [local(): pl.pallas_call(pair_kernel, out_shape=(shape((2, OWN), F32), shape((2, OW...]
where the time goes in v5:
time: 40.9 us; the launch traced here: 40.8 us
  Pallas kernels  40.2 us (98%)
  between operations  0.66 us (2%)
    pallas_call x1, Pallas kernels, local(): pl.pallas_call(histogram_kernel, out_shape=(shape((8, TILE), F32), shape(...  25.5 us
    pallas_call x1, Pallas kernels, local(): pl.pallas_call(prepare_kernel, out_shape=(shape((1, WIN), F32), shape((8,...  8.58 us
    pallas_call x1, Pallas kernels, local(): pl.pallas_call(pair_kernel, out_shape=(shape((2, OWN), F32), shape((2, OW...  5.5 us

profile of v5, /device:TPU:1, one launch (start us, length us, event | category | flops | bytes accessed | tf_op | source)
XLA Modules:
  0.0 40.8 jit_solution(18381399721437244161)
XLA Ops:
  0.6 8.6 %prepare.1 = (f32[1,3072]{1,0:T(1,128)S(1)}, f32[8,3072]{1,0:T(8,128)S(1)}, s32[8,128]{1,0:T(8,128)S(1)}, f32[256,1024]{1,0:T(8,128)S(1)}, f32[3072,128]{1,0:T(8,128)S(1)}, /*index=5*/f32[3072,128]{1,0:T(8,128)S(1)}) custom-call(f32[1,1024]{1,0:T(1,128)} %bitcast.8, s32[1,8192]{1,0:T(1,128)} %bitcast.7, s32[1,32]{1,0:T(1,128)} %lengths_in.1, ...), custom_call_target="tpu_custom_call" | custom-call | tf_op jit(solution)/shard_map/prepare/pallas_call | solution.py:594
  9.2 0.0 copy-start
  9.2 5.5 %pairs.1 = (f32[2,1024]{1,0:T(2,128)}, f32[2,1024]{1,0:T(2,128)S(1)}) custom-call(s32[8,128]{1,0:T(8,128)S(1)} %get-tuple-element.18.table, f32[1,3072]{1,0:T(1,128)S(1)} %get-tuple-element.19.window_in, f32[8,3072]{1,0:T(8,128)S(1)} %get-tuple-element.20.rows, f32[3072,128]{1,0:T(8,128)S(1)} %get-tuple-element.21.id_col, ...), custom_call_target="tpu_custom_call" | custom-call | tf_op jit(solution)/shard_map/pairs/pallas_call | solution.py:615
  14.7 0.0 copy-done
  14.7 25.5 %histograms.1 = (f32[8,128]{1,0:T(8,128)S(1)}, f32[1,1024]{1,0:T(1,128)S(1)}, f32[8,128]{1,0:T(8,128)S(1)}) custom-call(f32[2,1024]{1,0:T(2,128)S(1)} %get-tuple-element.24.lambdas, s32[1,1024]{1,0:T(1,128)S(1)} %bitcast.6, f32[256,1024]{1,0:T(8,128)S(1)} %get-tuple-element.25.bins_t), custom_call_target="tpu_custom_call" | custom-call | tf_op jit(solution)/shard_map/histograms/pallas_call | solution.py:625
  40.2 0.6 %finish.1 = (f32[8,128]{1,0:T(8,128)}, f32[1,1024]{1,0:T(1,128)}, f32[3,256]{1,0:T(4,128)}) custom-call(f32[8,128]{1,0:T(8,128)S(1)} %get-tuple-element.26.leaf_in, f32[1,1024]{1,0:T(1,128)S(1)} %get-tuple-element.27.step_in, f32[8,128]{1,0:T(8,128)S(1)} %get-tuple-element.28.hist_in), custom_call_target="tpu_custom_call" | custom-call | tf_op jit(solution)/shard_map/finish/pallas_call | solution.py:651
Async XLA Ops:
  9.2 5.5 %copy-start = (s32[1024]{0:T(1024)S(1)}, s32[1024]{0:T(1024)}, u32[]{:S(2)}) copy-start(s32[1024]{0:T(1024)} %param.8) | copy-start | bytes 12292

commit v6 on v5

--- a/solution.py
+++ b/solution.py
@@ -23,7 +23,8 @@
 SIDE = 4
 RING = 8
 GROUP = 8
-EARLY = 4
+FAR_FIRST = (4, 3, 5, 2, 6, 1, 7)
+EARLY = 6
 HI = 8
 LO = 32
 
@@ -325,15 +326,16 @@
             src_ref=source, dst_ref=target, send_sem=send, recv_sem=recv, device_id=device, device_id_type=MESH_ID)
 
     barrier = pltpu.get_barrier_semaphore()
-    pl.semaphore_signal(barrier, inc=1, device_id=(sibling, feat), device_id_type=MESH_ID)
+    for offset in FAR_FIRST[:3]:
+        pl.semaphore_signal(barrier, inc=1, device_id=(query, ring_peer(offset)), device_id_type=MESH_ID)
 
     @pl.loop(1, CHIPS)
     def _(offset):
         pl.semaphore_signal(barrier, inc=1, device_id=(chip_peer(offset) * 2 + core, feat), device_id_type=MESH_ID)
 
-    @pl.loop(1, RING)
-    def _(offset):
+    for offset in FAR_FIRST[3:]:
         pl.semaphore_signal(barrier, inc=1, device_id=(query, ring_peer(offset)), device_id_type=MESH_ID)
+    pl.semaphore_signal(barrier, inc=1, device_id=(sibling, feat), device_id_type=MESH_ID)
 
     grad, curv = lambdas[0:1, :], lambdas[1:2, :]
     leaf = leaves[...]
@@ -524,8 +526,7 @@
         peer = ring_peer(offset)
         return remote(chunk.at[peer], chunk_got.at[peer], chunk_send.at[peer], chunk_recv.at[peer], (query, peer))
 
-    @pl.loop(1, RING)
-    def _(offset):
+    for offset in FAR_FIRST:
         chunk_copy(offset).start()
 
     @pl.loop(1, RING)
@@ -552,12 +553,6 @@
         found = found + jnp.dot(piece, lane_hot, preferred_element_type=F32)
     step_out[...] = shrinkage * jnp.sum(jnp.where(in_row, found, 0.0), axis=0, keepdims=True)
 
-    def add_chunk(offset, total):
-        chunk_arrival(offset).wait_recv()
-        return total + chunk_got[ring_peer(offset)]
-
-    hist_out[...] = lax.fori_loop(1, RING, add_chunk, chunk[feat])
-
     leaf_back.wait_send()
     pair_copy(CHIPS - 1).wait_send()
 
@@ -570,6 +565,13 @@
     @pl.loop(1, RING)
     def _(offset):
         ring_copy(offset).wait_send()
+
+    total = chunk[feat]
+    for offset in reversed(FAR_FIRST):
+        chunk_arrival(offset).wait_recv()
+        total = total + chunk_got[ring_peer(offset)]
+    hist_out[...] = total
+    for offset in FAR_FIRST:
         chunk_copy(offset).wait_send()
 
 

time: 40.9 us -> 39.1 us (0.956)
  Pallas kernels: 40.2 us -> 38.5 us
    pallas_call x1, Pallas kernels: 25.5 us -> 22.7 us  [local(): pl.pallas_call(histogram_kernel, out_shape=(shape((8, TILE), F32), shape(...]
    pallas_call x1, Pallas kernels: 5.5 us -> 6.51 us  [local(): pl.pallas_call(pair_kernel, out_shape=(shape((2, OWN), F32), shape((2, OW...]
where the time goes in v6:
time: 39.1 us
  Pallas kernels  38.5 us (98%)
  between operations  0.66 us (2%)
    pallas_call x1, Pallas kernels, local(): pl.pallas_call(histogram_kernel, out_shape=(shape((8, TILE), F32), shape(...  22.7 us
    pallas_call x1, Pallas kernels, local(): pl.pallas_call(prepare_kernel, out_shape=(shape((1, WIN), F32), shape((8,...  8.58 us
    pallas_call x1, Pallas kernels, local(): pl.pallas_call(pair_kernel, out_shape=(shape((2, OWN), F32), shape((2, OW...  6.51 us

profile of v6, /device:TPU:1, one launch (start us, length us, event | category | flops | bytes accessed | tf_op | source)
XLA Modules:
  0.0 39.1 jit_solution(11437480255585764460)
XLA Ops:
  0.6 8.6 %prepare.1 = (f32[1,3072]{1,0:T(1,128)S(1)}, f32[8,3072]{1,0:T(8,128)S(1)}, s32[8,128]{1,0:T(8,128)S(1)}, f32[256,1024]{1,0:T(8,128)S(1)}, f32[3072,128]{1,0:T(8,128)S(1)}, /*index=5*/f32[3072,128]{1,0:T(8,128)S(1)}) custom-call(f32[1,1024]{1,0:T(1,128)} %bitcast.8, s32[1,8192]{1,0:T(1,128)} %bitcast.7, s32[1,32]{1,0:T(1,128)} %lengths_in.1, ...), custom_call_target="tpu_custom_call" | custom-call | tf_op jit(solution)/shard_map/prepare/pallas_call | solution.py:596
  9.2 0.0 copy-start
  9.2 6.5 %pairs.1 = (f32[2,1024]{1,0:T(2,128)}, f32[2,1024]{1,0:T(2,128)S(1)}) custom-call(s32[8,128]{1,0:T(8,128)S(1)} %get-tuple-element.18.table, f32[1,3072]{1,0:T(1,128)S(1)} %get-tuple-element.19.window_in, f32[8,3072]{1,0:T(8,128)S(1)} %get-tuple-element.20.rows, f32[3072,128]{1,0:T(8,128)S(1)} %get-tuple-element.21.id_col, ...), custom_call_target="tpu_custom_call" | custom-call | tf_op jit(solution)/shard_map/pairs/pallas_call | solution.py:617
  15.7 0.0 copy-done
  15.7 22.7 %histograms.1 = (f32[8,128]{1,0:T(8,128)S(1)}, f32[1,1024]{1,0:T(1,128)S(1)}, f32[8,128]{1,0:T(8,128)S(1)}) custom-call(f32[2,1024]{1,0:T(2,128)S(1)} %get-tuple-element.24.lambdas, s32[1,1024]{1,0:T(1,128)S(1)} %bitcast.6, f32[256,1024]{1,0:T(8,128)S(1)} %get-tuple-element.25.bins_t), custom_call_target="tpu_custom_call" | custom-call | tf_op jit(solution)/shard_map/histograms/pallas_call | solution.py:627
  38.5 0.6 %finish.1 = (f32[8,128]{1,0:T(8,128)}, f32[1,1024]{1,0:T(1,128)}, f32[3,256]{1,0:T(4,128)}) custom-call(f32[8,128]{1,0:T(8,128)S(1)} %get-tuple-element.26.leaf_in, f32[1,1024]{1,0:T(1,128)S(1)} %get-tuple-element.27.step_in, f32[8,128]{1,0:T(8,128)S(1)} %get-tuple-element.28.hist_in), custom_call_target="tpu_custom_call" | custom-call | tf_op jit(solution)/shard_map/finish/pallas_call | solution.py:653
Async XLA Ops:
  9.2 6.5 %copy-start = (s32[1024]{0:T(1024)S(1)}, s32[1024]{0:T(1024)}, u32[]{:S(2)}) copy-start(s32[1024]{0:T(1024)} %param.8) | copy-start | bytes 12292
